TPU v7x, 32 devices: a whole 2x2x4 slice. The times are simulated.
32 devices in a mesh: group: 16 (over z, y, x), member: 2 (over core).
Axes of the slice: x: 2, y: 2, z: 4, core: 2. Of those that a mesh axis runs over, the one named last changes fastest.
Arguments:
- residual: float32 [2, 256, 64, 128], P(None, 'group', 'member'), may hold values from -6 to 6
- horiz_vectors: float32 [2, 18, 18], replicated, may hold values from -1.5 to 1.5
- horiz_values: float32 [2, 18], replicated, may hold values from 0.2 to 4
- upward_eigen_tables: float32 [8, 18, 18], replicated, may hold values from -1.5 to 1.5
- upward_eigen_values: float32 [8, 18], replicated, may hold values from 0.2 to 4
- aggregate_map: int32 [16, 4, 8], P('group', 'member'), may hold values from 0 to 127, as said below
- coarse_inverse: float32 [128, 128], P('group', 'member')
Outputs:
- preconditioned: float32 [2, 256, 64, 128], P(None, 'group', 'member')
Inputs may be any that keep to these rules, and one draw needn't show every extreme that they name: `aggregate_map`: the aggregate of each element; an element's aggregate holds elements next to it; every aggregate holds some element.
All inputs are finite; a program needn't handle non-finite values.
Results may differ from a plain program's by a relative error of at most 0.0003.
Values sent between devices are 32-bit elements; how exact they have to be, the bound alone decides.
A program may use at most 64 MiB of HBM per device.

v0:
```python
import jax
import jax.numpy as jnp
import numpy as np
from jax import lax
from jax.sharding import PartitionSpec as P

ELEMENT_POINTS = 16


def with_halo(shard, sides, width):
    for axis, dim in sides:
        devices, length = (lax.axis_size(axis), shard.shape[dim])
        up = [(i, (i + 1) % devices) for i in range(devices)]
        down = [(j, i) for i, j in up]
        last = lax.slice_in_dim(shard, length - width, length, axis=dim)
        leading = lax.slice_in_dim(shard, 0, width, axis=dim)
        before = lax.ppermute(last, axis, up)
        after = lax.ppermute(leading, axis, down)
        shard = jnp.concatenate([before, shard, after], axis=dim)
    return shard


def build_boxes(padded, span, count_y, count_z):
    extent = span + 2
    upward_rows = np.array(
        [k * span + c for k in range(count_z) for c in range(extent)], dtype=np.int32
    )
    second_rows = np.array(
        [j * span + b for j in range(count_y) for b in range(extent)], dtype=np.int32
    )
    stacked = jnp.take(padded, jnp.asarray(upward_rows), axis=3)
    stacked = jnp.take(stacked, jnp.asarray(second_rows), axis=2)
    vector_count = padded.shape[0]
    stacked = stacked.reshape(vector_count, extent, count_y, extent, count_z, extent)
    stacked = jnp.transpose(stacked, (1, 3, 0, 2, 4, 5))
    return stacked.reshape(extent, extent, vector_count * count_y * count_z * extent)


def fdm_solve(
    boxes,
    horiz_vectors,
    horiz_values,
    upward_eigen_tables,
    upward_eigen_values,
    batch_rows,
    count_z,
):
    highest = lax.Precision.HIGHEST
    extent = boxes.shape[0]
    lanes = boxes.shape[2]
    block_eye = jnp.eye(count_z, dtype=jnp.float32)
    block_table = (block_eye[:, None, :, None] * upward_eigen_tables[:, :, None, :]).reshape(
        count_z * extent, count_z * extent
    )
    hat = jnp.einsum("xyl,xa->ayl", boxes, horiz_vectors[0], precision=highest)
    hat = jnp.einsum("ayl,yb->abl", hat, horiz_vectors[1], precision=highest)
    hat = jnp.dot(
        hat.reshape(-1, count_z * extent),
        block_table,
        precision=highest,
        preferred_element_type=jnp.float32,
    )
    denominator = (
        horiz_values[0][:, None, None, None, None]
        + horiz_values[1][None, :, None, None, None]
        + upward_eigen_values[None, None, None, :, :]
    )
    scaled = hat.reshape(extent, extent, batch_rows, count_z, extent) / denominator
    solved = jnp.dot(
        scaled.reshape(-1, count_z * extent),
        block_table.T,
        precision=highest,
        preferred_element_type=jnp.float32,
    )
    solved = solved.reshape(extent, extent, lanes)
    solved = jnp.einsum("abl,yb->ayl", solved, horiz_vectors[1], precision=highest)
    solved = jnp.einsum("ayl,xa->xyl", solved, horiz_vectors[0], precision=highest)
    return solved


def on_device(
    residual,
    horiz_vectors,
    horiz_values,
    upward_eigen_tables,
    upward_eigen_values,
    aggregate_map,
    coarse_inverse,
):
    vector_count, points_x, span_y, span_z = residual.shape
    count_y = span_y // ELEMENT_POINTS
    count_z = span_z // ELEMENT_POINTS
    extent = ELEMENT_POINTS + 2
    partition_weight = float(ELEMENT_POINTS) ** (-1.5)
    aggregate_labels = aggregate_map.reshape(-1)
    slice_cols = coarse_inverse.shape[1]
    total_aggregates = coarse_inverse.shape[0] * lax.axis_size("group")
    padded = with_halo(residual, (("group", 1), ("member", 2)), 1)
    padded = jnp.pad(padded, ((0, 0), (0, 0), (0, 0), (1, 1)))
    boxes = build_boxes(padded, ELEMENT_POINTS, count_y, count_z)
    solved = fdm_solve(
        boxes,
        horiz_vectors,
        horiz_values,
        upward_eigen_tables,
        upward_eigen_values,
        vector_count * count_y,
        count_z,
    )
    solved = solved.reshape(extent, extent, vector_count, count_y, count_z, extent)
    solved = solved[1:-1, 1:-1, :, :, :, 1:-1]
    subdomain_part = jnp.transpose(solved, (2, 0, 3, 1, 4, 5))
    element_totals = residual.reshape(
        vector_count, ELEMENT_POINTS, count_y, ELEMENT_POINTS, count_z, ELEMENT_POINTS
    ).sum(axis=(1, 3, 5))
    element_totals = element_totals.reshape(vector_count, -1)
    partial_rhs = (
        partition_weight
        * jax.ops.segment_sum(element_totals.T, aggregate_labels, num_segments=total_aggregates).T
    )
    whole_rhs = lax.psum(partial_rhs, ("group", "member"))
    share_rhs = lax.dynamic_slice_in_dim(
        whole_rhs, lax.axis_index("member") * slice_cols, slice_cols, 1
    )
    row_terms = jnp.dot(
        share_rhs,
        coarse_inverse.T,
        precision=lax.Precision.HIGHEST,
        preferred_element_type=jnp.float32,
    )
    row_values = lax.psum(row_terms, "member")
    coarse_full = lax.all_gather(row_values, "group", axis=1, tiled=True)
    update_term = partition_weight * jnp.take(coarse_full, aggregate_labels, axis=1)
    update_term = update_term.reshape(vector_count, 1, count_y, 1, count_z, 1)
    merged_result = subdomain_part + update_term
    return merged_result.reshape(vector_count, points_x, span_y, span_z)


def solution(mesh):
    in_specs = (
        P(None, "group", "member", None),
        P(),
        P(),
        P(),
        P(),
        P("group", "member", None),
        P("group", "member"),
    )
    out_specs = P(None, "group", "member", None)
    return jax.shard_map(
        on_device, mesh=mesh, in_specs=in_specs, out_specs=out_specs, check_vma=False
    )
```

profile of v0, /device:TPU:0, one launch (start us, length us, event | category | flops | bytes accessed | tf_op | source)
XLA Modules:
  0.0 194.3 jit_solution(9653250678119578751)
XLA Ops:
  0.0 0.0 copy-start
  0.0 0.8 fusion.18
  0.8 2.9 %collective-permute-start = (f32[2,1,32,128]{3,2,1,0:T(8,128)S(1)}, f32[2,1,32,128]{3,2,1,0:T(8,128)S(1)}, u32[]{:S(2)}, u32[]{:S(2)}) collective-permute-start(f32[2,1,32,128]{3,2,1,0:T(8,128)S(1)} %get-tuple-element.10), channel_id=1, source_target_pairs={{0,2},{2,4},{4,6},{6,8},{8,10},{10,12},{12,14},{14,16},{16,18},{18... | collective-permute-start | bytes 98312 | tf_op jit(solution)/shard_map/ppermute | solution.py:17
  3.8 4.1 %collective-permute-start.1 = (f32[2,1,32,128]{3,2,1,0:T(8,128)S(1)}, f32[2,1,32,128]{3,2,1,0:T(8,128)S(1)}, u32[]{:S(2)}, u32[]{:S(2)}) collective-permute-start(f32[2,1,32,128]{3,2,1,0:T(8,128)S(1)} %get-tuple-element.9), channel_id=1, source_target_pairs={{2,0},{4,2},{6,4},{8,6},{10,8},{12,10},{14,12},{16,14},{18,16},{20... | collective-permute-start | bytes 98312 | tf_op jit(solution)/shard_map/ppermute | solution.py:18
  7.8 0.8 broadcast_in_dim_reshape.3
  8.6 0.7 compare_and_fusion.1
  9.3 0.7 pad_clamp_fusion.2
  9.9 0.7 pad_clamp_fusion.1
  10.6 0.8 fusion.19
  11.4 0.8 slice_bitcast_fusion.1
  12.2 1.0 copy.68
  13.2 0.1 broadcast_add_fusion.1
  13.3 2.1 %broadcast_add_fusion = f32[18,18,8,18]{3,1,2,0:T(8,128)} fusion(f32[8,18]{1,0:T(8,128)} %param.13, f32[18,18]{1,0:T(8,128)S(1)} %broadcast_add_fusion.1), kind=kLoop, calls=%fused_computation.17 | loop fusion | flops 46656 | bytes 188496 | tf_op jit(solution)/shard_map/add | solution.py:64
  15.4 0.1 broadcast_multiply_fusion
  15.5 0.1 reshape.191
  15.6 0.1 copy.93
  15.7 0.1 copy.94
  15.8 0.2 mul.49
  16.0 0.0 collective-permute-done
  16.1 0.0 collective-permute-done.1
  16.2 0.1 collective-permute-start.2
  16.3 0.6 collective-permute-start.3
  16.9 0.1 copy-done.3
  17.0 0.1 reduce_sum.14
  17.1 0.1 reduce_sum.18
  17.2 0.1 reshape.163
  17.3 0.1 copy.75
  17.4 0.7 scatter_custom_fusion
  18.1 38.1 %psum.14 = f32[2,128]{0,1:T(8,128)S(1)} all-reduce(f32[2,128]{0,1:T(8,128)S(1)} %multiply_bitcast_fusion), channel_id=1, replica_groups=mesh['group'=16,'member'=2] {'group','member'}, use_global_device_ids=true, to_apply=%region_3.4 | all-reduce | flops 256 | bytes 2048 | tf_op jit(solution)/shard_map/psum | solution.py:121
  56.2 0.2 fusion.5
  56.4 2.5 %psum.15 = f32[2,8]{1,0:T(2,128)S(1)} all-reduce(f32[2,8]{1,0:T(2,128)S(1)} %fusion.5), channel_id=1, replica_groups=mesh['group'=16,'member'=2] {'member'}, use_global_device_ids=true, to_apply=%region_4.5 | all-reduce | flops 16 | bytes 128 | tf_op jit(solution)/shard_map/psum | solution.py:131
  58.9 39.7 %all-gather = f32[16,8,2]{1,2,0:T(2,128)S(1)} all-gather(f32[1,8,2]{1,2,0:T(2,128)S(1)} %bitcast.83), channel_id=1, replica_groups=mesh['group'=16,'member'=2] {'group'}, dimensions={0}, use_global_device_ids=true | all-gather | bytes 1088 | tf_op jit(solution)/shard_map/all_gather | solution.py:132
  98.5 0.2 copy.76
  98.7 0.6 gather_fusion.2
  99.3 0.1 copy.89
  99.4 3.3 %copy.59 = f32[2,18,32,128]{2,0,3,1:T(2,128)S(1)} copy(f32[2,18,32,128]{3,2,1,0:T(8,128)} %copy-done.3) | data formatting | bytes 1179648 | tf_op jit(solution)/shard_map/concatenate | solution.py:19
  102.7 0.0 collective-permute-done.2
  102.7 2.5 %copy.58 = f32[2,18,1,128]{2,0,3,1:T(2,128)} copy(f32[2,18,1,128]{3,0,2,1:T(2,128)S(1)} %collective-permute-done.2) | data formatting | bytes 36864 | tf_op jit(solution)/shard_map/ppermute | solution.py:17
  105.2 0.0 collective-permute-done.3
  105.2 2.4 %copy.60 = f32[2,18,1,128]{2,0,3,1:T(2,128)} copy(f32[2,18,1,128]{3,0,2,1:T(2,128)S(1)} %collective-permute-done.3) | data formatting | bytes 36864 | tf_op jit(solution)/shard_map/ppermute | solution.py:18
  107.7 7.4 %select_maximum_fusion = f32[2,18,34,130]{2,0,3,1:T(2,128)} fusion(f32[2,18,1,128]{2,0,3,1:T(2,128)} %copy.60, f32[2,18,32,128]{2,0,3,1:T(2,128)S(1)} %copy.59, f32[2,18,1,128]{2,0,3,1:T(2,128)} %copy.58), kind=kLoop, calls=%fused_computation.8 | loop fusion | flops 1272960 | bytes 1263168 | tf_op jit(solution)/shard_map/concatenate | solution.py:19
  115.0 15.3 %gather_fusion = f32[144,2,18,34]{3,1,2,0:T(2,128)S(1)} fusion(f32[2,18,34,130]{2,0,3,1:T(2,128)} %select_maximum_fusion, s32[1024]{0:T(1024)S(1)} %pad_clamp_fusion.2), kind=kCustom, calls=%fused_computation | custom fusion | bytes 1410624 | tf_op jit(solution)/shard_map/jit(_take)/gather | solution.py:31
  130.4 3.6 %copy.61 = f32[2,18,34,144]{3,0,2,1:T(2,128)} copy(f32[2,18,34,144]{2,0,1,3:T(2,128)S(1)} %bitcast.76) | data formatting | bytes 1410048 | tf_op jit(solution)/shard_map/jit(_take)/gather | solution.py:31
  134.0 3.4 %gather_fusion.1 = f32[36,2,18,144]{3,1,2,0:T(2,128)S(1)} fusion(f32[2,18,34,144]{3,0,2,1:T(2,128)} %copy.61, s32[1024]{0:T(1024)S(1)} %pad_clamp_fusion.1), kind=kCustom, calls=%fused_computation.1 | custom fusion | bytes 1493136 | tf_op jit(solution)/shard_map/jit(_take)/gather | solution.py:32
  137.4 0.5 copy.62
  137.9 4.4 %gather.18 = f32[2,18,2,18,8,18]{5,4,0,3,2,1:T(8,128)} reshape(f32[2,18,36,144]{3,0,2,1:T(2,128)S(1)} %copy.62) | data formatting | bytes 1492992 | tf_op jit(solution)/shard_map/jit(_take)/gather | solution.py:32
  142.2 5.6 %copy.84 = f32[18,18,2,2,8,18]{5,4,3,2,0,1:T(8,128)} copy(f32[18,18,2,2,8,18]{5,4,2,1,3,0:T(8,128)} %bitcast.75) | data formatting | bytes 1492992 | tf_op jit(solution)/shard_map/reshape | solution.py:36
  147.8 5.7 %reshape.206 = f32[18,18,576]{2,0,1:T(8,128)S(1)} reshape(f32[18,18,2,2,8,18]{5,4,3,2,0,1:T(8,128)} %copy.84) | data formatting | bytes 1492992 | tf_op jit(solution)/shard_map/reshape | solution.py:36
  153.5 1.0 convolution_bitcast_fusion.3
  154.6 1.2 convolution_bitcast_fusion.2
  155.8 2.0 %dot_general.34 = f32[18,18,4,144]{3,2,1,0:T(4,128)} reshape(f32[18,18,576]{2,1,0:T(8,128)S(1)} %convolution_bitcast_fusion.2) | data formatting | bytes 1492992 | tf_op jit(solution)/shard_map/dot_general | solution.py:57
  157.8 0.0 copy-done.2
  157.8 7.6 %broadcast_divide_fusion = f32[18,18,4,8,18]{4,1,3,2,0:T(8,128)S(1)} fusion(f32[18,18,8,18]{3,1,2,0:T(8,128)S(1)} %copy-done.2, f32[18,18,4,144,1]{3,2,1,0,4:T(4,128)} %bitcast.78, f32[8,18,144,1,1]{2,1,0,3,4:T(8,128)S(1)} %reshape.203), kind=kOutput, calls=%fused_computation.7 | convolution fusion | flops 322672896 | bytes 1762560 | tf_op jit(solution)/shard_map/dot_general | solution.py:57
  165.4 3.2 %copy.70 = f32[18,18,4,8,18]{4,3,2,1,0:T(8,128)} copy(f32[18,18,4,8,18]{4,1,3,2,0:T(8,128)S(1)} %broadcast_divide_fusion) | data formatting | bytes 1492992 | tf_op jit(solution)/shard_map/div | solution.py:68
  168.7 4.0 %reshape.159 = f32[1296,144]{1,0:T(8,128)S(1)} reshape(f32[18,18,4,8,18]{4,3,2,1,0:T(8,128)} %copy.70) | data formatting | bytes 1492992 | tf_op jit(solution)/shard_map/reshape | solution.py:70
  172.7 1.2 fusion.20
  173.9 0.9 reshape.160
  174.8 1.1 convolution_bitcast_fusion.1
  175.9 1.2 convolution_bitcast_fusion
  177.1 7.4 %reshape.161 = f32[18,18,2,2,8,18]{5,4,3,2,0,1:T(8,128)} reshape(f32[18,18,576]{2,0,1:T(8,128)S(1)} %convolution_bitcast_fusion) | data formatting | bytes 1492992 | tf_op jit(solution)/shard_map/reshape | solution.py:110
  184.5 3.3 %fusion = f32[2,16,2,16,8,16]{5,4,2,0,1,3:T(8,128)S(1)} fusion(f32[18,18,2,2,8,18]{5,4,3,2,0,1:T(8,128)} %reshape.161, f32[2,2,8]{2,1,0:T(2,128)S(1)} %select_multiply_fusion), kind=kLoop, calls=%fused_computation.6 | loop fusion | flops 131072 | bytes 1048704 | tf_op jit(solution)/shard_map/add | solution.py:135
  187.9 0.0 copy-start.1
  187.9 2.5 %copy.78 = f32[2,16,2,16,8,16]{5,4,3,2,1,0:T(8,128)} copy(f32[2,16,2,16,8,16]{5,4,2,0,1,3:T(8,128)S(1)} %fusion) | data formatting | bytes 1048576 | tf_op jit(solution)/shard_map/add | solution.py:135
  190.4 3.9 %reshape.164 = f32[2,16,32,128]{3,2,1,0:T(8,128)} reshape(f32[2,16,2,16,8,16]{5,4,3,2,1,0:T(8,128)} %copy.78) | data formatting | bytes 1048576 | tf_op jit(solution)/shard_map/reshape | solution.py:136
  (20 shorter events, 0.2 us)
Async XLA Ops:
  0.0 56.2 %copy-start = (f32[8,64]{1,0:T(8,128)S(1)}, f32[8,64]{1,0:T(8,128)}, u32[]{:S(2)}) copy-start(f32[8,64]{1,0:T(8,128)} %param.15) | copy-start | bytes 6148
  0.0 15.5 %copy-start.5 = (s32[1,2,8]{2,1,0:T(2,128)S(1)}, s32[1,2,8]{2,1,0:T(2,128)}, u32[]{:S(2)}) copy-start(s32[1,2,8]{2,1,0:T(2,128)} %param.14) | copy-start | bytes 196
  0.8 15.2 %collective-permute-start = (f32[2,1,32,128]{3,2,1,0:T(8,128)S(1)}, f32[2,1,32,128]{3,2,1,0:T(8,128)S(1)}, u32[]{:S(2)}, u32[]{:S(2)}) collective-permute-start(f32[2,1,32,128]{3,2,1,0:T(8,128)S(1)} %get-tuple-element.10), channel_id=1, source_target_pairs={{0,2},{2,4},{4,6},{6,8},{8,10},{10,12},{12,14},{14,16},{16,18},{18... | collective-permute-start | bytes 98312 | tf_op jit(solution)/shard_map/ppermute | solution.py:17
  3.8 12.4 %collective-permute-start.1 = (f32[2,1,32,128]{3,2,1,0:T(8,128)S(1)}, f32[2,1,32,128]{3,2,1,0:T(8,128)S(1)}, u32[]{:S(2)}, u32[]{:S(2)}) collective-permute-start(f32[2,1,32,128]{3,2,1,0:T(8,128)S(1)} %get-tuple-element.9), channel_id=1, source_target_pairs={{2,0},{4,2},{6,4},{8,6},{10,8},{12,10},{14,12},{16,14},{18,16},{20... | collective-permute-start | bytes 98312 | tf_op jit(solution)/shard_map/ppermute | solution.py:18
  13.3 2.8 %copy-start.4 = (f32[2,16,32,128]{3,2,1,0:T(8,128)S(1)}, f32[2,16,32,128]{3,2,1,0:T(8,128)}, u32[]{:S(2)}) copy-start(f32[2,16,32,128]{3,2,1,0:T(8,128)} %param.9) | copy-start | bytes 1572868
  16.1 0.8 copy-start.3
  16.2 86.5 %collective-permute-start.2 = (f32[2,18,1,128]{3,0,2,1:T(2,128)S(1)}, f32[2,18,1,128]{3,0,2,1:T(2,128)S(1)}, u32[]{:S(2)}, u32[]{:S(2)}) collective-permute-start(f32[2,18,1,128]{3,0,2,1:T(2,128)S(1)} %copy.91), channel_id=1, source_target_pairs={{0,1},{1,0},{2,3},{3,2},{4,5},{5,4},{6,7},{7,6},{8,9},{9,8},{10,11... | collective-permute-start | bytes 55304 | tf_op jit(solution)/shard_map/ppermute | solution.py:17
  16.3 88.9 %collective-permute-start.3 = (f32[2,18,1,128]{3,0,2,1:T(2,128)S(1)}, f32[2,18,1,128]{3,0,2,1:T(2,128)S(1)}, u32[]{:S(2)}, u32[]{:S(2)}) collective-permute-start(f32[2,18,1,128]{3,0,2,1:T(2,128)S(1)} %copy.92), channel_id=1, source_target_pairs={{1,0},{0,1},{3,2},{2,3},{5,4},{4,5},{7,6},{6,7},{9,8},{8,9},{11,10... | collective-permute-start | bytes 55304 | tf_op jit(solution)/shard_map/ppermute | solution.py:18
  155.8 2.0 %copy-start.2 = (f32[18,18,8,18]{3,1,2,0:T(8,128)S(1)}, f32[18,18,8,18]{3,1,2,0:T(8,128)}, u32[]{:S(2)}) copy-start(f32[18,18,8,18]{3,1,2,0:T(8,128)} %broadcast_add_fusion) | copy-start | bytes 559876
  187.9 6.5 %copy-start.1 = (f32[8,64]{1,0:T(8,128)S(1)}, f32[8,64]{1,0:T(8,128)}, u32[]{:S(2)}) copy-start(f32[8,64]{1,0:T(8,128)} %param.15) | copy-start | bytes 6148
where the time goes:
time: 195 us; the launch traced here: 194 us
  blocking collectives  80.3 us (41%)
  local copies, waits for them, and re-layouts  76.7 us (39%)
  other arithmetic  15.9 us (8%)
  matrix products  13.5 us (7%)
  starting transfers between devices  7.62 us (4%)
    all_gather x1, blocking collectives, on_device(): coarse_full = lax.all_gather(row_values, 'group', axis=1, tiled=True)  39.7 us
    psum x1, blocking collectives, on_device(): whole_rhs = lax.psum(partial_rhs, ('group', 'member'))  38.1 us
    gather x2, local copies, waits for them, and re-layouts, build_boxes(): stacked = jnp.take(padded, jnp.asarray(upward_rows), axis=3)  18.9 us
    reshape x2, local copies, waits for them, and re-layouts, build_boxes(): stacked.reshape(extent, extent, vector_count * count_y * count_z * extent)  11.3 us
    gather x3, local copies, waits for them, and re-layouts, build_boxes(): stacked = jnp.take(stacked, jnp.asarray(second_rows), axis=2)  8.23 us
    dot_general x1, matrix products, fdm_solve(): jnp.dot(hat.reshape(-1, count_z * extent), block_table, precision=highest...  7.64 us
    reshape x1, local copies, waits for them, and re-layouts, on_device(): solved.reshape(extent, extent, vector_count, count_y, count_z, extent)  7.43 us
    concatenate x1, other arithmetic, with_halo(): shard = jnp.concatenate([before, shard, after], axis=dim)  7.37 us
  transfers between devices with their start and end apart: 4, of which 0 were waited for; matrix products, arithmetic and copies ran while one was open for 8% of the time, Pallas kernels for 0%

commit v1 on v0

v1 whole, which is shorter than its diff:
```python
import functools

import jax
import jax.numpy as jnp
from jax import lax
from jax.experimental import pallas as pl
from jax.experimental.pallas import tpu as pltpu
from jax.sharding import PartitionSpec as P

SPAN = 16
EXTENT = SPAN + 2
MAIN = SPAN * SPAN
TAIL = 24
REST = 2 * SPAN + 2 * TAIL
ROWS = MAIN + REST
WEIGHT = float(SPAN) ** (-1.5)
MESH = pl.DeviceIdType.MESH
F32 = jnp.float32
BF16 = jnp.bfloat16


def iota(shape, dim):
    return lax.broadcasted_iota(jnp.int32, shape, dim)


def dot(a, b):
    return jnp.dot(a, b, precision=lax.Precision.HIGHEST, preferred_element_type=F32)


def dot_t(a, b):
    dims = (((1,), (1,)), ((), ()))
    return lax.dot_general(
        a, b, dims, precision=lax.Precision.HIGHEST, preferred_element_type=F32
    )


def bdot(a, b):
    return jnp.dot(a, b, preferred_element_type=F32)


def split(a):
    hi = a.astype(BF16)
    return hi, (a - hi.astype(F32)).astype(BF16)


def rest_of(lane):
    r = lane - MAIN
    r = jnp.where(r >= 2 * REST, r - 2 * REST, jnp.where(r >= REST, r - REST, r))
    t = r - 2 * SPAN
    tail = (t >= 0) & (lane < MAIN + 3 * REST)
    second = t >= TAIL
    return r, tail, second, jnp.where(second, t - TAIL, t)


def point_index(lane):
    r, tail, second, along = rest_of(lane)
    side = jnp.where(r >= SPAN, EXTENT - 1, 0)
    tail_x = jnp.where(
        along < SPAN,
        along + 1,
        jnp.where(along == SPAN, 0, jnp.where(along == SPAN + 1, EXTENT - 1, -1)),
    )
    x = jnp.where(lane < MAIN, 1 + lane // SPAN, jnp.where(tail, tail_x, side))
    y = jnp.where(
        lane < MAIN,
        1 + lane % SPAN,
        jnp.where(tail, jnp.where(second, EXTENT - 1, 0), 1 + r % SPAN),
    )
    return x, y


def mode_index(lane):
    r, tail, second, along = rest_of(lane)
    a = jnp.where(lane < MAIN, lane // SPAN, jnp.where(tail, along, SPAN + r // SPAN))
    b = jnp.where(
        lane < MAIN,
        lane % SPAN,
        jnp.where(tail, jnp.where(second, SPAN + 1, SPAN), r % SPAN),
    )
    return a, b


def store_split(ref, table):
    hi, lo = split(table)
    rows = table.shape[0]
    ref[:, 0:MAIN] = hi[:, :MAIN]
    ref[:, MAIN : 2 * MAIN] = hi[:, :MAIN]
    ref[:, 2 * MAIN : 3 * MAIN] = lo[:, :MAIN]
    lane = iota((rows, MAIN), 1)
    wide = table[:, MAIN:]
    top = wide.astype(BF16).astype(F32)
    mixed = jnp.where(lane < 2 * REST, top, wide - top)
    ref[:, 3 * MAIN :] = jnp.where(lane < 3 * REST, mixed, 0.0).astype(BF16)


def kernel(
    groups,
    members,
    direct,
    res_hbm,
    hvec_hbm,
    hval_hbm,
    ztab_hbm,
    zval_hbm,
    agg_hbm,
    inv_hbm,
    out_hbm,
    res,
    hvec,
    hval,
    ztab,
    zval,
    agg,
    inv,
    out,
    hpad,
    zpad,
    apad,
    ysend,
    csend,
    xrecv,
    yrecv,
    crecv,
    msg,
    box,
    fwd,
    bwd,
    recip,
    zfwd,
    zbwd,
    part,
    in_sem,
    out_sem,
    halo_send,
    halo_recv,
    all_send,
    all_recv,
):
    vectors, _, span_y, span_z = res.shape
    count_y = span_y // SPAN
    count_z = span_z // SPAN
    modes_z = count_z * EXTENT
    total = groups * members
    g = lax.axis_index("group")
    m = lax.axis_index("member")
    me = g * members + m

    def peer(step):
        other = lax.rem(me + step, total)
        return (other // members, lax.rem(other, members))

    def shifted(dx, dy):
        return (lax.rem(g + dx + groups, groups), lax.rem(m + dy + members, members))

    barrier = pltpu.get_barrier_semaphore()
    around = [(dx, dy) for dx in (-1, 0, 1) for dy in (-1, 0, 1) if dx or dy]
    if direct:

        def greet(step, carry):
            pl.semaphore_signal(barrier, inc=1, device_id=peer(step), device_id_type=MESH)
            return carry

        lax.fori_loop(1, total, greet, 0)
    else:
        for dx, dy in around:
            pl.semaphore_signal(
                barrier, inc=1, device_id=shifted(dx, dy), device_id_type=MESH
            )

    loads = [
        pltpu.make_async_copy(src, dst, in_sem.at[i])
        for i, (src, dst) in enumerate(
            [
                (res_hbm, res),
                (agg_hbm, agg),
                (inv_hbm, inv),
                (hvec_hbm, hvec),
                (hval_hbm, hval),
                (ztab_hbm, ztab),
                (zval_hbm, zval),
            ]
        )
    ]
    for load in loads:
        load.start()
    hpad[...] = jnp.zeros_like(hpad)
    zpad[...] = jnp.zeros_like(zpad)
    apad[...] = jnp.zeros_like(apad)
    for load in loads:
        load.wait()

    for v in range(vectors):
        ysend[0, v] = res[v, :, span_y - 1, :]
        ysend[1, v] = res[v, :, 0, :]
    for cx in range(2):
        for cy in range(2):
            for v in range(vectors):
                row = cx * 4 + cy * 2 + v
                y_at = (span_y - 1) * cy
                csend[row : row + 1, :] = res[v, (SPAN - 1) * cx, y_at : y_at + 1, :]

    row8 = iota((8, span_z), 0)
    if direct:
        spread = (iota((count_z, span_z), 1) // SPAN == iota((count_z, span_z), 0)).astype(F32)
        labels = dot(agg[0].astype(F32), spread)
        half = inv.shape[1]
        row_id = iota((2 * half, span_z), 0)
        rhs = jnp.zeros((8, 2 * half), F32)
        for j in range(count_y):
            sums = jnp.zeros((8, span_z), F32)
            for v in range(vectors):
                tot = jnp.sum(res[v, :, j * SPAN : (j + 1) * SPAN, :], axis=0)
                tot = jnp.sum(tot, axis=0, keepdims=True)
                sums = sums + jnp.where(row8 % 4 == v, tot, 0.0)
            label = labels[j : j + 1, :]
            low = (label == (row_id - half).astype(F32)) & (row_id >= half)
            high = (label == row_id.astype(F32)) & (row_id >= half)
            rhs = rhs + jnp.where(
                row8 < 4, dot_t(sums, low.astype(F32)), dot_t(sums, high.astype(F32))
            )
        apad[:, 0:half] = inv[...]
        mine = apad[...] + WEIGHT * rhs
        msg[me] = mine
        box[...] = mine

    halo = []

    def send(src, dst, dx, dy):
        i = len(halo)
        copy = pltpu.make_async_remote_copy(
            src_ref=src,
            dst_ref=dst,
            send_sem=halo_send.at[i],
            recv_sem=halo_recv.at[i],
            device_id=shifted(dx, dy),
            device_id_type=MESH,
        )
        halo.append(copy)

    send(res.at[:, SPAN - 1], xrecv.at[0], 1, 0)
    send(res.at[:, 0], xrecv.at[1], -1, 0)
    corner_dy = (1,) if members == 2 else (1, -1)
    for ix, dx in enumerate((1, -1)):
        for iy, dy in enumerate(corner_dy):
            send(csend, crecv.at[ix, iy], dx, dy)
    send(ysend.at[0], yrecv.at[0], 0, 1)
    send(ysend.at[1], yrecv.at[1], 0, -1)

    pl.semaphore_wait(barrier, total - 1 if direct else len(around))
    for copy in halo:
        copy.start()
    if direct:

        def share(step, carry):
            pltpu.make_async_remote_copy(
                src_ref=box,
                dst_ref=msg.at[me],
                send_sem=all_send,
                recv_sem=all_recv,
                device_id=peer(step),
                device_id_type=MESH,
            ).start()
            return carry

        lax.fori_loop(1, total, share, 0)

    hpad[:, 0:EXTENT, 0:EXTENT] = hvec[...]
    wide = 2 * MAIN
    lane = iota((TAIL, wide), 1)
    row = iota((TAIL, wide), 0)
    eye = (iota((TAIL, 128), 0) == iota((TAIL, 128), 1)).astype(F32)
    px, py = point_index(lane)
    xe = dot(dot_t(eye, hpad[0]), (px == row).astype(F32))
    ye = dot(dot_t(eye, hpad[1]), (py == row).astype(F32))
    body = xe[:EXTENT][:, None, :] * ye[:SPAN][None, :, :]
    table = jnp.concatenate(
        [
            body.reshape(EXTENT * SPAN, wide),
            xe * ye[SPAN : SPAN + 1, :],
            xe * ye[SPAN + 1 : SPAN + 2, :],
        ],
        axis=0,
    )
    store_split(fwd, table)
    ma, mb = mode_index(lane)
    xb = dot(hpad[0, 1 : SPAN + 1, 0:TAIL], (ma == row).astype(F32))
    yb = dot(hpad[1, 1 : SPAN + 1, 0:TAIL], (mb == row).astype(F32))
    store_split(bwd, (xb[:, None, :] * yb[None, :, :]).reshape(MAIN, wide))

    zpad[:, 0:EXTENT, 0:EXTENT] = ztab[...]
    tiled = (iota((128, modes_z), 1) % EXTENT == iota((128, modes_z), 0)).astype(F32)
    stacked = count_z * TAIL
    diag = dot(zpad[...].reshape(stacked, 128), tiled)
    own = iota((stacked, modes_z), 1) // EXTENT == iota((stacked, modes_z), 0) // TAIL
    diag = jnp.where(own, diag, 0.0)
    zz = iota((span_z, stacked), 0)
    layer = iota((span_z, stacked), 1) // TAIL
    inner = iota((span_z, stacked), 1) % TAIL
    band = ((zz == SPAN * layer - 1 + inner) & (inner < EXTENT)).astype(F32)
    near = ((zz // SPAN == layer) & (inner == zz % SPAN + 1)).astype(F32)
    hi, lo = split(dot(band, diag))
    zfwd[0:span_z, :] = hi
    zfwd[span_z : 2 * span_z, :] = lo
    zfwd[2 * span_z : 3 * span_z, :] = hi
    eye_z = (iota((modes_z, modes_z), 0) == iota((modes_z, modes_z), 1)).astype(F32)
    hi, lo = split(dot_t(eye_z, dot(near, diag)))
    zbwd[:, 0:span_z] = hi
    zbwd[:, span_z : 2 * span_z] = lo

    lane_h = iota((ROWS, EXTENT), 1)
    row_h = iota((ROWS, EXTENT), 0)
    t = row_h - EXTENT * SPAN
    along = jnp.where(t >= TAIL, t - TAIL, t)
    a_of = jnp.where(t < 0, row_h // SPAN, along)
    b_of = jnp.where(t < 0, row_h % SPAN, jnp.where(t >= TAIL, SPAN + 1, SPAN))
    column = jnp.where(lane_h == a_of, hval[0:1, :], 0.0)
    column = column + jnp.where(lane_h == b_of, hval[1:2, :], 0.0)
    column = jnp.sum(column, axis=1, keepdims=True)
    levels = dot(zval[...], tiled[:EXTENT])
    level_own = iota((count_z, modes_z), 1) // EXTENT == iota((count_z, modes_z), 0)
    levels = jnp.sum(jnp.where(level_own, levels, 0.0), axis=0, keepdims=True)
    recip[...] = 1.0 / (column + levels)

    for v in range(vectors):
        field = jnp.concatenate(
            [
                res[v, :, j * SPAN : (j + 1) * SPAN, :].reshape(MAIN, span_z)
                for j in range(count_y)
            ],
            axis=1,
        )
        hi, lo = split(field)
        part[v] = bdot(fwd[:, 0 : 3 * MAIN], jnp.concatenate([hi, lo, hi], axis=0))

    for copy in halo:
        copy.wait_recv()

    rim_row = iota((8, span_z), 0)
    solved = []
    for v in range(vectors):
        rests = []
        for j in range(count_y):
            rows = slice(j * SPAN, (j + 1) * SPAN)
            pieces = [xrecv[0, v, rows, :], xrecv[1, v, rows, :]]
            for side in range(2):
                at = j * SPAN - 1 if side == 0 else (j + 1) * SPAN
                if 0 <= at < span_y:
                    pieces.append(res[v, :, at, :])
                    before = xrecv[0, v, at : at + 1, :]
                    after = xrecv[1, v, at : at + 1, :]
                else:
                    pieces.append(yrecv[side, v])
                    iy = 0 if members == 2 else side
                    cy = 1 - side
                    r0, r1 = 4 + cy * 2 + v, cy * 2 + v
                    before = crecv[0, iy, r0 : r0 + 1, :]
                    after = crecv[1, iy, r1 : r1 + 1, :]
                pieces.append(
                    jnp.where(rim_row == 0, before, jnp.where(rim_row == 1, after, 0.0))
                )
            rests.append(jnp.concatenate(pieces, axis=0))
        hi, lo = split(jnp.concatenate(rests, axis=1))
        hat = part[v] + bdot(fwd[:, 3 * MAIN :][:, : 3 * REST], jnp.concatenate([hi, lo, hi], axis=0))
        backs = []
        for j in range(count_y):
            hi, lo = split(hat[:, j * span_z : (j + 1) * span_z])
            spectral = bdot(jnp.concatenate([hi, hi, lo], axis=1), zfwd[...]) * recip[...]
            hi, lo = split(spectral)
            both = bdot(hi, zbwd[...])
            backs.append(
                both[:, :span_z] + both[:, span_z:] + bdot(lo, zbwd[:, 0:span_z])
            )
        solved.append(jnp.concatenate(backs, axis=1))

    updates = None
    if direct:
        done = pltpu.make_async_copy(
            msg.at[pl.ds(0, total - 1)], msg.at[pl.ds(0, total - 1)], all_recv
        )
        done.wait()
        blocks = msg[...]
        whole = pltpu.roll(jnp.sum(blocks, axis=0), half, 1)
        lane8 = iota((8, 2 * half), 1)
        whole = jnp.where(lane8 < half, whole, 0.0)
        blocks = blocks.reshape(groups, members, 8, 2 * half)
        answer = jnp.zeros((8, groups * 8), F32)
        for part_m in range(members):
            chosen = jnp.where(row8 // 4 == part_m, whole, 0.0)
            answer = answer + dot_t(chosen, blocks[:, part_m].reshape(groups * 8, 2 * half))
        updates = []
        for j in range(count_y):
            pick = (labels[j : j + 1, :] == row_id.astype(F32)).astype(F32)
            updates.append(WEIGHT * dot(answer, pick))

    stores = []
    for v in range(vectors):
        hi, lo = split(solved[v])
        result = bdot(
            bwd[:, 0 : 3 * MAIN],
            jnp.concatenate([hi[:MAIN], lo[:MAIN], hi[:MAIN]], axis=0),
        ) + bdot(
            bwd[:, 3 * MAIN :][:, : 3 * REST],
            jnp.concatenate([hi[MAIN:], lo[MAIN:], hi[MAIN:]], axis=0),
        )
        for j in range(count_y):
            piece = result[:, j * span_z : (j + 1) * span_z]
            if direct:
                piece = piece + (updates[j][v : v + 1, :] + updates[j][4 + v : 5 + v, :])
            out[v, :, j * SPAN : (j + 1) * SPAN, :] = piece.reshape(SPAN, SPAN, span_z)
        store = pltpu.make_async_copy(out.at[v], out_hbm.at[v], out_sem.at[v])
        store.start()
        stores.append(store)

    for copy in halo:
        copy.wait_send()
    if direct:
        pltpu.make_async_copy(
            msg.at[pl.ds(0, total - 1)], msg.at[pl.ds(0, total - 1)], all_send
        ).wait()
    for store in stores:
        store.wait()


def on_device(
    residual,
    horiz_vectors,
    horiz_values,
    upward_eigen_tables,
    upward_eigen_values,
    aggregate_map,
    coarse_inverse,
):
    groups = lax.axis_size("group")
    members = lax.axis_size("member")
    vectors, points_x, span_y, span_z = residual.shape
    count_y = span_y // SPAN
    count_z = span_z // SPAN
    total = groups * members
    rows, cols = coarse_inverse.shape
    direct = total <= 64 and members == 2 and rows == 8 and cols == 64 and groups * 8 == 128
    operands = (
        residual,
        horiz_vectors,
        horiz_values,
        upward_eigen_tables,
        upward_eigen_values,
        aggregate_map,
        coarse_inverse,
    )
    corners = 1 if members == 2 else 2
    halos = 4 + 2 * corners
    dma = pltpu.SemaphoreType.DMA
    scratch = [pltpu.VMEM(a.shape, a.dtype) for a in operands]
    scratch += [
        pltpu.VMEM(residual.shape, F32),
        pltpu.VMEM((2, TAIL, 128), F32),
        pltpu.VMEM((count_z, TAIL, 128), F32),
        pltpu.VMEM((8, 128), F32),
        pltpu.VMEM((2, vectors, SPAN, span_z), F32),
        pltpu.VMEM((8, span_z), F32),
        pltpu.VMEM((2, vectors, span_y, span_z), F32),
        pltpu.VMEM((2, vectors, SPAN, span_z), F32),
        pltpu.VMEM((2, corners, 8, span_z), F32),
        pltpu.VMEM((total if direct else 1, 8, 128), F32),
        pltpu.VMEM((8, 128), F32),
        pltpu.VMEM((ROWS, 4 * MAIN), BF16),
        pltpu.VMEM((MAIN, 4 * MAIN), BF16),
        pltpu.VMEM((ROWS, count_z * EXTENT), F32),
        pltpu.VMEM((3 * span_z, count_z * EXTENT), BF16),
        pltpu.VMEM((count_z * EXTENT, 2 * span_z), BF16),
        pltpu.VMEM((vectors, ROWS, count_y * span_z), F32),
        dma((len(operands),)),
        dma((vectors,)),
        dma((halos,)),
        dma((halos,)),
        dma,
        dma,
    ]
    result = pl.pallas_call(
        functools.partial(kernel, groups, members, direct),
        out_shape=jax.ShapeDtypeStruct(residual.shape, F32),
        in_specs=[pl.BlockSpec(memory_space=pl.ANY)] * len(operands),
        out_specs=pl.BlockSpec(memory_space=pl.ANY),
        scratch_shapes=scratch,
        compiler_params=pltpu.CompilerParams(
            collective_id=0, has_side_effects=True, vmem_limit_bytes=40 * 1024 * 1024
        ),
        cost_estimate=pl.CostEstimate(
            flops=2 * 10**9, bytes_accessed=2**20, transcendentals=0
        ),
    )(*operands)
    if direct:
        return result
    totals = residual.reshape(vectors, SPAN, count_y, SPAN, count_z, SPAN).sum(axis=(1, 3, 5))
    labels = aggregate_map.reshape(-1)
    partial_rhs = WEIGHT * jax.ops.segment_sum(
        totals.reshape(vectors, -1).T, labels, num_segments=rows * groups
    ).T
    whole_rhs = lax.psum(partial_rhs, ("group", "member"))
    share = lax.dynamic_slice_in_dim(whole_rhs, lax.axis_index("member") * cols, cols, 1)
    row_values = lax.psum(dot(share, coarse_inverse.T), "member")
    coarse = lax.all_gather(row_values, "group", axis=1, tiled=True)
    update = WEIGHT * jnp.take(coarse, labels, axis=1)
    update = update.reshape(vectors, 1, count_y, 1, count_z, 1)
    split_up = (vectors, SPAN, count_y, SPAN, count_z, SPAN)
    return (result.reshape(split_up) + update).reshape(residual.shape)


def solution(mesh):
    in_specs = (
        P(None, "group", "member", None),
        P(),
        P(),
        P(),
        P(),
        P("group", "member", None),
        P("group", "member"),
    )
    out_specs = P(None, "group", "member", None)
    return jax.shard_map(
        on_device, mesh=mesh, in_specs=in_specs, out_specs=out_specs, check_vma=False
    )
```

time: 195 us -> 18.3 us (0.09)
  blocking collectives: 80.3 us -> 0 us
  local copies, waits for them, and re-layouts: 76.7 us -> 3.52 us
  other arithmetic: 15.9 us -> 0 us
  Pallas kernels: 0 us -> 14.4 us
  matrix products: 13.5 us -> 0 us
  starting transfers between devices: 7.62 us -> 0 us
    psum x2 -> x0, blocking collectives: 40.6 us -> none  [the longest x1 38.1 us: on_device(): whole_rhs = lax.psum(partial_rhs, ('group', 'member'))]
    all_gather x1 -> x0, blocking collectives: 39.7 us -> none  [on_device(): coarse_full = lax.all_gather(row_values, 'group', axis=1, tiled=True)]
    gather x7 -> x0, local copies, waits for them, and re-layouts: 27.8 us -> none  [the longest x2 18.9 us: build_boxes(): stacked = jnp.take(padded, jnp.asarray(upward_rows), axis=3)]
    reshape x7 -> x0, local copies, waits for them, and re-layouts: 27.7 us -> none  [the longest x2 11.3 us: build_boxes(): stacked.reshape(extent, extent, vector_count * count_y * count_z * extent)]
    pallas_call x0 -> x1, Pallas kernels: none -> 14.4 us  [on_device(): pl.pallas_call(functools.partial(kernel, groups, members, direct), out_sh...]
    dot_general x7 -> x0, matrix products: 13.5 us -> none  [the longest x1 7.64 us: fdm_solve(): jnp.dot(hat.reshape(-1, count_z * extent), block_table, precision=highest...]
    ppermute x4 -> x0, starting transfers between devices: 7.62 us -> none  [the longest x2 4.61 us: with_halo(): after = lax.ppermute(leading, axis, down)]
    concatenate x1 -> x0, other arithmetic: 7.37 us -> none  [with_halo(): shard = jnp.concatenate([before, shard, after], axis=dim)]
  transfers between devices with their start and end apart: 4 -> 0, of which waited for: 0 -> 0; matrix products, arithmetic and copies ran while one was open for 8% -> 0% of each run, Pallas kernels for 0% -> 0%
where the time goes in v1:
time: 18.3 us; the launch traced here: 18 us
  Pallas kernels  14.4 us (79%)
  local copies, waits for them, and re-layouts  3.52 us (19%)
    pallas_call x1, Pallas kernels, on_device(): pl.pallas_call(functools.partial(kernel, groups, members, direct), out_sh...  14.4 us
    unnamed x13, local copies, waits for them, and re-layouts  3.52 us

profile of v1, /device:TPU:0, one launch (start us, length us, event | category | flops | bytes accessed | tf_op | source)
XLA Modules:
  0.0 18.0 jit_solution(10762262538172840962)
XLA Ops:
  0.0 0.7 %copy.8.hvec_hbm = f32[2,18,18]{2,1,0:T(8,128)S(1)} copy(f32[2,18,18]{2,0,1:T(2,128)} %param.8) | data formatting | bytes 5184 | tf_op args[1]
  0.7 0.0 copy-start.1
  0.7 0.0 copy-start.2
  0.7 0.0 copy-start.3
  0.7 0.0 copy-start.4
  0.7 0.9 %copy.9.ztab_hbm = f32[8,18,18]{2,1,0:T(8,128)S(1)} copy(f32[8,18,18]{2,0,1:T(8,128)} %param.10) | data formatting | bytes 20736 | tf_op args[3]
  1.7 0.0 copy-done.1
  1.7 0.0 copy-done.2
  1.7 0.0 copy-done.3
  1.7 0.0 copy-done.4
  1.7 0.0 copy-start
  1.7 1.0 %copy-done = f32[2,16,32,128]{3,2,1,0:T(8,128)S(1)} copy-done((f32[2,16,32,128]{3,2,1,0:T(8,128)S(1)}, f32[2,16,32,128]{3,2,1,0:T(8,128)}, u32[]{:S(2)}) %copy-start) | copy-done | bytes 524312
  2.8 14.4 %shard_map.73 = f32[2,16,32,128]{3,2,1,0:T(8,128)S(1)} custom-call(f32[2,16,32,128]{3,2,1,0:T(8,128)S(1)} %copy-done, f32[2,18,18]{2,1,0:T(8,128)S(1)} %copy.8.hvec_hbm, f32[2,18]{1,0:T(2,128)S(1)} %copy-done.3, f32[8,18,18]{2,1,0:T(8,128)S(1)} %copy.9.ztab_hbm, f32[8,18]{1,0:T(8,128)S(1)} %copy-done.1, s32[1,2,8]{2,1,0:T(2,128)S(1)} %copy-done.4, ...), custom_call_target="tpu_custom_call" | custom-call | flops 2000000000 | bytes 1048576 | tf_op jit(solution)/shard_map/pallas_call | solution.py:479
  17.2 0.8 %copy.11 = f32[2,16,32,128]{3,2,1,0:T(8,128)} copy(f32[2,16,32,128]{3,2,1,0:T(8,128)S(1)} %shard_map.73) | data formatting | bytes 1048576
Async XLA Ops:
  0.7 1.0 %copy-start.1 = (f32[8,18]{1,0:T(8,128)S(1)}, f32[8,18]{1,0:T(8,128)}, u32[]{:S(2)}) copy-start(f32[8,18]{1,0:T(8,128)} %zval_hbm.1) | copy-start | bytes 1732
  0.7 1.0 %copy-start.2 = (f32[8,64]{1,0:T(8,128)S(1)}, f32[8,64]{1,0:T(8,128)}, u32[]{:S(2)}) copy-start(f32[8,64]{1,0:T(8,128)} %inv_hbm.1) | copy-start | bytes 6148
  0.7 1.0 %copy-start.3 = (f32[2,18]{1,0:T(2,128)S(1)}, f32[2,18]{1,0:T(2,128)}, u32[]{:S(2)}) copy-start(f32[2,18]{1,0:T(2,128)} %hval_hbm.1) | copy-start | bytes 436
  0.7 1.0 %copy-start.4 = (s32[1,2,8]{2,1,0:T(2,128)S(1)}, s32[1,2,8]{2,1,0:T(2,128)}, u32[]{:S(2)}) copy-start(s32[1,2,8]{2,1,0:T(2,128)} %agg_hbm.1) | copy-start | bytes 196
  1.7 1.0 %copy-start = (f32[2,16,32,128]{3,2,1,0:T(8,128)S(1)}, f32[2,16,32,128]{3,2,1,0:T(8,128)}, u32[]{:S(2)}) copy-start(f32[2,16,32,128]{3,2,1,0:T(8,128)} %res_hbm.1) | copy-start | bytes 1572868

commit v2 on v1

--- a/solution.py
+++ b/solution.py
@@ -38,9 +38,41 @@
     return jnp.dot(a, b, preferred_element_type=F32)
 
 
+def bdot_t(a, b):
+    dims = (((1,), (1,)), ((), ()))
+    return lax.dot_general(a, b, dims, preferred_element_type=F32)
+
+
 def split(a):
     hi = a.astype(BF16)
     return hi, (a - hi.astype(F32)).astype(BF16)
+
+
+def choose(a, hot):
+    hi, lo = split(a)
+    return bdot(hi, hot) + bdot(lo, hot)
+
+
+def place(hot, a):
+    hi, lo = split(a)
+    return bdot(hot, hi) + bdot(hot, lo)
+
+
+def turn(hot, a):
+    hi, lo = split(a)
+    return bdot_t(hot, hi) + bdot_t(hot, lo)
+
+
+def hot(condition):
+    return condition.astype(F32).astype(BF16)
+
+
+def high(i):
+    return lax.shift_right_logical(i, 4)
+
+
+def low(i):
+    return i & (SPAN - 1)
 
 
 def rest_of(lane):
@@ -60,22 +92,22 @@
         along + 1,
         jnp.where(along == SPAN, 0, jnp.where(along == SPAN + 1, EXTENT - 1, -1)),
     )
-    x = jnp.where(lane < MAIN, 1 + lane // SPAN, jnp.where(tail, tail_x, side))
+    x = jnp.where(lane < MAIN, 1 + high(lane), jnp.where(tail, tail_x, side))
     y = jnp.where(
         lane < MAIN,
-        1 + lane % SPAN,
-        jnp.where(tail, jnp.where(second, EXTENT - 1, 0), 1 + r % SPAN),
+        1 + low(lane),
+        jnp.where(tail, jnp.where(second, EXTENT - 1, 0), 1 + low(r)),
     )
     return x, y
 
 
 def mode_index(lane):
     r, tail, second, along = rest_of(lane)
-    a = jnp.where(lane < MAIN, lane // SPAN, jnp.where(tail, along, SPAN + r // SPAN))
+    a = jnp.where(lane < MAIN, high(lane), jnp.where(tail, along, SPAN + high(r)))
     b = jnp.where(
         lane < MAIN,
-        lane % SPAN,
-        jnp.where(tail, jnp.where(second, SPAN + 1, SPAN), r % SPAN),
+        low(lane),
+        jnp.where(tail, jnp.where(second, SPAN + 1, SPAN), low(r)),
     )
     return a, b
 
@@ -114,7 +146,6 @@
     inv,
     out,
     hpad,
-    zpad,
     apad,
     ysend,
     csend,
@@ -145,22 +176,32 @@
     m = lax.axis_index("member")
     me = g * members + m
 
-    def peer(step):
-        other = lax.rem(me + step, total)
-        return (other // members, lax.rem(other, members))
+    def wrap(i, n):
+        return jnp.where(i >= n, i - n, i)
 
     def shifted(dx, dy):
-        return (lax.rem(g + dx + groups, groups), lax.rem(m + dy + members, members))
+        return (wrap(g + dx % groups, groups), wrap(m + dy % members, members))
+
+    def for_peers(act):
+        for dy in range(1, members):
+            act(shifted(0, dy))
+
+        def step(dx, carry):
+            other = wrap(g + dx, groups)
+            for dy in range(members):
+                act((other, wrap(m + dy, members)))
+            return carry
+
+        lax.fori_loop(1, groups, step, 0)
 
     barrier = pltpu.get_barrier_semaphore()
     around = [(dx, dy) for dx in (-1, 0, 1) for dy in (-1, 0, 1) if dx or dy]
     if direct:
-
-        def greet(step, carry):
-            pl.semaphore_signal(barrier, inc=1, device_id=peer(step), device_id_type=MESH)
-            return carry
-
-        lax.fori_loop(1, total, greet, 0)
+        for_peers(
+            lambda device: pl.semaphore_signal(
+                barrier, inc=1, device_id=device, device_id_type=MESH
+            )
+        )
     else:
         for dx, dy in around:
             pl.semaphore_signal(
@@ -184,10 +225,45 @@
     for load in loads:
         load.start()
     hpad[...] = jnp.zeros_like(hpad)
-    zpad[...] = jnp.zeros_like(zpad)
     apad[...] = jnp.zeros_like(apad)
-    for load in loads:
+    for load in loads[1:]:
         load.wait()
+
+    hpad[0, 0:EXTENT, 0:EXTENT] = hvec[:, 0, :]
+    hpad[1, 0:EXTENT, 0:EXTENT] = hvec[:, 1, :]
+    wide = 2 * MAIN
+    lane = iota((1, wide), 1)
+    row = iota((TAIL, wide), 0)
+    eye = hot(iota((TAIL, 128), 0) == iota((TAIL, 128), 1))
+    px, py = point_index(lane)
+    xe = choose(turn(eye, hpad[0]), hot(px == row))
+    ye = choose(turn(eye, hpad[1]), hot(py == row))
+    body = xe[:EXTENT][:, None, :] * ye[:SPAN][None, :, :]
+    table = jnp.concatenate(
+        [
+            body.reshape(EXTENT * SPAN, wide),
+            xe * ye[SPAN : SPAN + 1, :],
+            xe * ye[SPAN + 1 : SPAN + 2, :],
+        ],
+        axis=0,
+    )
+    store_split(fwd, table)
+    ma, mb = mode_index(lane)
+    xb = choose(hpad[0, 1 : SPAN + 1, 0:TAIL], hot(ma == row))
+    yb = choose(hpad[1, 1 : SPAN + 1, 0:TAIL], hot(mb == row))
+    store_split(bwd, (xb[:, None, :] * yb[None, :, :]).reshape(MAIN, wide))
+
+    row8 = iota((8, span_z), 0)
+    if direct:
+        half = inv.shape[1]
+        spread = hot(high(iota((count_z, span_z), 1)) == iota((count_z, span_z), 0))
+        labels = dot(agg[0].astype(F32), spread.astype(F32))
+        row_id = iota((2 * half, span_z), 0).astype(F32)
+        member_of = jnp.concatenate(
+            [hot(labels[j : j + 1, :] == row_id) for j in range(count_y)], axis=1
+        )
+        apad[:, 0:half] = inv[...]
+    loads[0].wait()
 
     for v in range(vectors):
         ysend[0, v] = res[v, :, span_y - 1, :]
@@ -199,27 +275,20 @@
                 y_at = (span_y - 1) * cy
                 csend[row : row + 1, :] = res[v, (SPAN - 1) * cx, y_at : y_at + 1, :]
 
-    row8 = iota((8, span_z), 0)
-    if direct:
-        spread = (iota((count_z, span_z), 1) // SPAN == iota((count_z, span_z), 0)).astype(F32)
-        labels = dot(agg[0].astype(F32), spread)
-        half = inv.shape[1]
-        row_id = iota((2 * half, span_z), 0)
-        rhs = jnp.zeros((8, 2 * half), F32)
+    if direct:
+        sums = []
         for j in range(count_y):
-            sums = jnp.zeros((8, span_z), F32)
+            placed = jnp.zeros((8, span_z), F32)
             for v in range(vectors):
                 tot = jnp.sum(res[v, :, j * SPAN : (j + 1) * SPAN, :], axis=0)
                 tot = jnp.sum(tot, axis=0, keepdims=True)
-                sums = sums + jnp.where(row8 % 4 == v, tot, 0.0)
-            label = labels[j : j + 1, :]
-            low = (label == (row_id - half).astype(F32)) & (row_id >= half)
-            high = (label == row_id.astype(F32)) & (row_id >= half)
-            rhs = rhs + jnp.where(
-                row8 < 4, dot_t(sums, low.astype(F32)), dot_t(sums, high.astype(F32))
-            )
-        apad[:, 0:half] = inv[...]
-        mine = apad[...] + WEIGHT * rhs
+                placed = placed + jnp.where((row8 & 3) == v, tot, 0.0)
+            sums.append(placed)
+        hi, lo = split(jnp.concatenate(sums, axis=1))
+        rhs = WEIGHT * (bdot_t(hi, member_of) + bdot_t(lo, member_of))
+        lane8 = iota((8, 2 * half), 1)
+        rhs = jnp.where(row8 < 4, pltpu.roll(rhs, half, 1), rhs)
+        mine = apad[...] + jnp.where(lane8 < half, 0.0, rhs)
         msg[me] = mine
         box[...] = mine
 
@@ -250,60 +319,35 @@
     for copy in halo:
         copy.start()
     if direct:
-
-        def share(step, carry):
-            pltpu.make_async_remote_copy(
+        for_peers(
+            lambda device: pltpu.make_async_remote_copy(
                 src_ref=box,
                 dst_ref=msg.at[me],
                 send_sem=all_send,
                 recv_sem=all_recv,
-                device_id=peer(step),
+                device_id=device,
                 device_id_type=MESH,
             ).start()
-            return carry
-
-        lax.fori_loop(1, total, share, 0)
-
-    hpad[:, 0:EXTENT, 0:EXTENT] = hvec[...]
-    wide = 2 * MAIN
-    lane = iota((TAIL, wide), 1)
-    row = iota((TAIL, wide), 0)
-    eye = (iota((TAIL, 128), 0) == iota((TAIL, 128), 1)).astype(F32)
-    px, py = point_index(lane)
-    xe = dot(dot_t(eye, hpad[0]), (px == row).astype(F32))
-    ye = dot(dot_t(eye, hpad[1]), (py == row).astype(F32))
-    body = xe[:EXTENT][:, None, :] * ye[:SPAN][None, :, :]
-    table = jnp.concatenate(
-        [
-            body.reshape(EXTENT * SPAN, wide),
-            xe * ye[SPAN : SPAN + 1, :],
-            xe * ye[SPAN + 1 : SPAN + 2, :],
-        ],
-        axis=0,
-    )
-    store_split(fwd, table)
-    ma, mb = mode_index(lane)
-    xb = dot(hpad[0, 1 : SPAN + 1, 0:TAIL], (ma == row).astype(F32))
-    yb = dot(hpad[1, 1 : SPAN + 1, 0:TAIL], (mb == row).astype(F32))
-    store_split(bwd, (xb[:, None, :] * yb[None, :, :]).reshape(MAIN, wide))
-
-    zpad[:, 0:EXTENT, 0:EXTENT] = ztab[...]
-    tiled = (iota((128, modes_z), 1) % EXTENT == iota((128, modes_z), 0)).astype(F32)
-    stacked = count_z * TAIL
-    diag = dot(zpad[...].reshape(stacked, 128), tiled)
-    own = iota((stacked, modes_z), 1) // EXTENT == iota((stacked, modes_z), 0) // TAIL
-    diag = jnp.where(own, diag, 0.0)
+        )
+
+    stacked = count_z * EXTENT
+    mode = iota((1, modes_z), 1)
+    mode_layer = mode // EXTENT
+    mode_inner = mode - EXTENT * mode_layer
+    tiled = hot(mode_inner == iota((EXTENT, modes_z), 0))
+    diag = choose(ztab[...].reshape(stacked, EXTENT), tiled)
+    diag = jnp.where(mode_layer == iota((stacked, modes_z), 0) % count_z, diag, 0.0)
     zz = iota((span_z, stacked), 0)
-    layer = iota((span_z, stacked), 1) // TAIL
-    inner = iota((span_z, stacked), 1) % TAIL
-    band = ((zz == SPAN * layer - 1 + inner) & (inner < EXTENT)).astype(F32)
-    near = ((zz // SPAN == layer) & (inner == zz % SPAN + 1)).astype(F32)
-    hi, lo = split(dot(band, diag))
+    layer = iota((1, stacked), 1) % count_z
+    inner = iota((1, stacked), 1) // count_z
+    band = hot(zz == SPAN * layer - 1 + inner)
+    near = hot((high(zz) == layer) & (inner == low(zz) + 1))
+    hi, lo = split(place(band, diag))
     zfwd[0:span_z, :] = hi
     zfwd[span_z : 2 * span_z, :] = lo
     zfwd[2 * span_z : 3 * span_z, :] = hi
-    eye_z = (iota((modes_z, modes_z), 0) == iota((modes_z, modes_z), 1)).astype(F32)
-    hi, lo = split(dot_t(eye_z, dot(near, diag)))
+    eye_z = hot(iota((modes_z, modes_z), 0) == iota((modes_z, modes_z), 1))
+    hi, lo = split(turn(eye_z, place(near, diag)))
     zbwd[:, 0:span_z] = hi
     zbwd[:, span_z : 2 * span_z] = lo
 
@@ -311,13 +355,13 @@
     row_h = iota((ROWS, EXTENT), 0)
     t = row_h - EXTENT * SPAN
     along = jnp.where(t >= TAIL, t - TAIL, t)
-    a_of = jnp.where(t < 0, row_h // SPAN, along)
-    b_of = jnp.where(t < 0, row_h % SPAN, jnp.where(t >= TAIL, SPAN + 1, SPAN))
+    a_of = jnp.where(t < 0, high(row_h), along)
+    b_of = jnp.where(t < 0, low(row_h), jnp.where(t >= TAIL, SPAN + 1, SPAN))
     column = jnp.where(lane_h == a_of, hval[0:1, :], 0.0)
     column = column + jnp.where(lane_h == b_of, hval[1:2, :], 0.0)
     column = jnp.sum(column, axis=1, keepdims=True)
-    levels = dot(zval[...], tiled[:EXTENT])
-    level_own = iota((count_z, modes_z), 1) // EXTENT == iota((count_z, modes_z), 0)
+    levels = dot(zval[...], tiled.astype(F32))
+    level_own = mode_layer == iota((count_z, modes_z), 0)
     levels = jnp.sum(jnp.where(level_own, levels, 0.0), axis=0, keepdims=True)
     recip[...] = 1.0 / (column + levels)
 
@@ -380,17 +424,13 @@
         done.wait()
         blocks = msg[...]
         whole = pltpu.roll(jnp.sum(blocks, axis=0), half, 1)
-        lane8 = iota((8, 2 * half), 1)
         whole = jnp.where(lane8 < half, whole, 0.0)
         blocks = blocks.reshape(groups, members, 8, 2 * half)
         answer = jnp.zeros((8, groups * 8), F32)
         for part_m in range(members):
             chosen = jnp.where(row8 // 4 == part_m, whole, 0.0)
             answer = answer + dot_t(chosen, blocks[:, part_m].reshape(groups * 8, 2 * half))
-        updates = []
-        for j in range(count_y):
-            pick = (labels[j : j + 1, :] == row_id.astype(F32)).astype(F32)
-            updates.append(WEIGHT * dot(answer, pick))
+        updates = WEIGHT * choose(answer, member_of)
 
     stores = []
     for v in range(vectors):
@@ -405,7 +445,8 @@
         for j in range(count_y):
             piece = result[:, j * span_z : (j + 1) * span_z]
             if direct:
-                piece = piece + (updates[j][v : v + 1, :] + updates[j][4 + v : 5 + v, :])
+                lanes = slice(j * span_z, (j + 1) * span_z)
+                piece = piece + (updates[v : v + 1, lanes] + updates[4 + v : 5 + v, lanes])
             out[v, :, j * SPAN : (j + 1) * SPAN, :] = piece.reshape(SPAN, SPAN, span_z)
         store = pltpu.make_async_copy(out.at[v], out_hbm.at[v], out_sem.at[v])
         store.start()
@@ -440,9 +481,9 @@
     direct = total <= 64 and members == 2 and rows == 8 and cols == 64 and groups * 8 == 128
     operands = (
         residual,
-        horiz_vectors,
+        jnp.transpose(horiz_vectors, (1, 0, 2)),
         horiz_values,
-        upward_eigen_tables,
+        jnp.transpose(upward_eigen_tables, (1, 0, 2)),
         upward_eigen_values,
         aggregate_map,
         coarse_inverse,
@@ -454,7 +495,6 @@
     scratch += [
         pltpu.VMEM(residual.shape, F32),
         pltpu.VMEM((2, TAIL, 128), F32),
-        pltpu.VMEM((count_z, TAIL, 128), F32),
         pltpu.VMEM((8, 128), F32),
         pltpu.VMEM((2, vectors, SPAN, span_z), F32),
         pltpu.VMEM((8, span_z), F32),
@@ -479,11 +519,11 @@
     result = pl.pallas_call(
         functools.partial(kernel, groups, members, direct),
         out_shape=jax.ShapeDtypeStruct(residual.shape, F32),
-        in_specs=[pl.BlockSpec(memory_space=pl.ANY)] * len(operands),
+        in_specs=[pl.BlockSpec(memory_space=pltpu.HBM)] * len(operands),
         out_specs=pl.BlockSpec(memory_space=pl.ANY),
         scratch_shapes=scratch,
         compiler_params=pltpu.CompilerParams(
-            collective_id=0, has_side_effects=True, vmem_limit_bytes=40 * 1024 * 1024
+            collective_id=0, has_side_effects=True, vmem_limit_bytes=60 * 1024 * 1024
         ),
         cost_estimate=pl.CostEstimate(
             flops=2 * 10**9, bytes_accessed=2**20, transcendentals=0

time: 18.3 us -> 17.2 us (0.940)
  local copies, waits for them, and re-layouts: 3.52 us -> 1.87 us
  Pallas kernels: 14.4 us -> 15.1 us
    unnamed x13 -> x1, local copies, waits for them, and re-layouts: 3.52 us -> 1.87 us
    pallas_call x1, Pallas kernels: 14.4 us -> 15.1 us  [on_device(): pl.pallas_call(functools.partial(kernel, groups, members, direct), out_sh...]
where the time goes in v2:
time: 17.2 us; the launch traced here: 17 us
  Pallas kernels  15.1 us (88%)
  local copies, waits for them, and re-layouts  1.87 us (11%)
    pallas_call x1, Pallas kernels, on_device(): pl.pallas_call(functools.partial(kernel, groups, members, direct), out_sh...  15.1 us
    unnamed x1, local copies, waits for them, and re-layouts  1.87 us

profile of v2, /device:TPU:0, one launch (start us, length us, event | category | flops | bytes accessed | tf_op | source)
XLA Modules:
  0.0 17.0 jit_solution(11213764283261381057)
XLA Ops:
  0.0 15.1 %shard_map.73 = f32[2,16,32,128]{3,2,1,0:T(8,128)} custom-call(f32[2,16,32,128]{3,2,1,0:T(8,128)} %res_hbm.1, f32[18,2,18]{2,1,0:T(2,128)} %bitcast.3, f32[2,18]{1,0:T(2,128)} %hval_hbm.1, f32[18,8,18]{2,1,0:T(8,128)} %bitcast.2, f32[8,18]{1,0:T(8,128)} %zval_hbm.1, s32[1,2,8]{2,1,0:T(2,128)} %agg_hbm.1, f32[8,64]{1,0:T(8,128)} %inv_hbm.1), custom_call_target="tpu_custom_call" | custom-call | flops 2000000000 | bytes 1048576 | tf_op jit(solution)/shard_map/pallas_call | solution.py:519
  15.1 1.9 %copy.9 = f32[2,16,32,128]{3,2,1,0:T(8,128)} copy(f32[2,16,32,128]{3,2,1,0:T(8,128)} %shard_map.73) | data formatting | bytes 1048576

commit v3 on v2

--- a/solution.py
+++ b/solution.py
@@ -14,6 +14,7 @@
 REST = 2 * SPAN + 2 * TAIL
 ROWS = MAIN + REST
 WEIGHT = float(SPAN) ** (-1.5)
+PLANES = 4
 MESH = pl.DeviceIdType.MESH
 F32 = jnp.float32
 BF16 = jnp.bfloat16
@@ -182,32 +183,23 @@
     def shifted(dx, dy):
         return (wrap(g + dx % groups, groups), wrap(m + dy % members, members))
 
-    def for_peers(act):
-        for dy in range(1, members):
-            act(shifted(0, dy))
-
-        def step(dx, carry):
-            other = wrap(g + dx, groups)
-            for dy in range(members):
-                act((other, wrap(m + dy, members)))
-            return carry
-
-        lax.fori_loop(1, groups, step, 0)
+    plane = groups // PLANES
+    first = g // plane * plane
+    inside = g - first
+
+    def near_peers():
+        peers = [(g, wrap(m + dy, members)) for dy in range(1, members)]
+        for dx in range(1, plane):
+            other = first + wrap(inside + dx, plane)
+            peers += [(other, wrap(m + dy, members)) for dy in range(members)]
+        return peers
+
+    def far_peers():
+        return [(wrap(g + plane * dz, groups), m) for dz in range(1, PLANES)]
+
+    near_total = plane * members
 
     barrier = pltpu.get_barrier_semaphore()
-    around = [(dx, dy) for dx in (-1, 0, 1) for dy in (-1, 0, 1) if dx or dy]
-    if direct:
-        for_peers(
-            lambda device: pl.semaphore_signal(
-                barrier, inc=1, device_id=device, device_id_type=MESH
-            )
-        )
-    else:
-        for dx, dy in around:
-            pl.semaphore_signal(
-                barrier, inc=1, device_id=shifted(dx, dy), device_id_type=MESH
-            )
-
     loads = [
         pltpu.make_async_copy(src, dst, in_sem.at[i])
         for i, (src, dst) in enumerate(
@@ -224,20 +216,44 @@
     ]
     for load in loads:
         load.start()
+    corner_dy = (1,) if members == 2 else (1, -1)
+    around = [(1, 0), (-1, 0), (0, 1)] + [(0, -1)] * (members > 2)
+    around += [(dx, dy) for dx in (1, -1) for dy in corner_dy]
+    partners = [shifted(dx, dy) for dx, dy in around]
+    if direct:
+        partners += near_peers() + far_peers()
+    for device in partners:
+        pl.semaphore_signal(barrier, inc=1, device_id=device, device_id_type=MESH)
     hpad[...] = jnp.zeros_like(hpad)
     apad[...] = jnp.zeros_like(apad)
-    for load in loads[1:]:
-        load.wait()
-
-    hpad[0, 0:EXTENT, 0:EXTENT] = hvec[:, 0, :]
-    hpad[1, 0:EXTENT, 0:EXTENT] = hvec[:, 1, :]
+
     wide = 2 * MAIN
     lane = iota((1, wide), 1)
     row = iota((TAIL, wide), 0)
     eye = hot(iota((TAIL, 128), 0) == iota((TAIL, 128), 1))
     px, py = point_index(lane)
-    xe = choose(turn(eye, hpad[0]), hot(px == row))
-    ye = choose(turn(eye, hpad[1]), hot(py == row))
+    ma, mb = mode_index(lane)
+    px, py, ma, mb = [hot(i == row) for i in (px, py, ma, mb)]
+    stacked = count_z * EXTENT
+    mode = iota((1, modes_z), 1)
+    mode_layer = mode // EXTENT
+    mode_inner = mode - EXTENT * mode_layer
+    tiled = hot(mode_inner == iota((EXTENT, modes_z), 0))
+    zz = iota((span_z, stacked), 0)
+    layer = iota((1, stacked), 1) % count_z
+    inner = iota((1, stacked), 1) // count_z
+    band = hot(zz == SPAN * layer - 1 + inner)
+    near = hot((high(zz) == layer) & (inner == low(zz) + 1))
+    eye_z = hot(iota((modes_z, modes_z), 0) == iota((modes_z, modes_z), 1))
+    row8 = iota((8, span_z), 0)
+    spread = hot(high(iota((count_z, span_z), 1)) == iota((count_z, span_z), 0))
+    for load in loads[1:]:
+        load.wait()
+
+    hpad[0, 0:EXTENT, 0:EXTENT] = hvec[:, 0, :]
+    hpad[1, 0:EXTENT, 0:EXTENT] = hvec[:, 1, :]
+    xe = choose(turn(eye, hpad[0]), px)
+    ye = choose(turn(eye, hpad[1]), py)
     body = xe[:EXTENT][:, None, :] * ye[:SPAN][None, :, :]
     table = jnp.concatenate(
         [
@@ -248,15 +264,12 @@
         axis=0,
     )
     store_split(fwd, table)
-    ma, mb = mode_index(lane)
-    xb = choose(hpad[0, 1 : SPAN + 1, 0:TAIL], hot(ma == row))
-    yb = choose(hpad[1, 1 : SPAN + 1, 0:TAIL], hot(mb == row))
+    xb = choose(hpad[0, 1 : SPAN + 1, 0:TAIL], ma)
+    yb = choose(hpad[1, 1 : SPAN + 1, 0:TAIL], mb)
     store_split(bwd, (xb[:, None, :] * yb[None, :, :]).reshape(MAIN, wide))
 
-    row8 = iota((8, span_z), 0)
     if direct:
         half = inv.shape[1]
-        spread = hot(high(iota((count_z, span_z), 1)) == iota((count_z, span_z), 0))
         labels = dot(agg[0].astype(F32), spread.astype(F32))
         row_id = iota((2 * half, span_z), 0).astype(F32)
         member_of = jnp.concatenate(
@@ -308,45 +321,36 @@
 
     send(res.at[:, SPAN - 1], xrecv.at[0], 1, 0)
     send(res.at[:, 0], xrecv.at[1], -1, 0)
-    corner_dy = (1,) if members == 2 else (1, -1)
     for ix, dx in enumerate((1, -1)):
         for iy, dy in enumerate(corner_dy):
             send(csend, crecv.at[ix, iy], dx, dy)
     send(ysend.at[0], yrecv.at[0], 0, 1)
     send(ysend.at[1], yrecv.at[1], 0, -1)
 
-    pl.semaphore_wait(barrier, total - 1 if direct else len(around))
+    pl.semaphore_wait(barrier, len(partners))
     for copy in halo:
         copy.start()
     if direct:
-        for_peers(
-            lambda device: pltpu.make_async_remote_copy(
+        near_copies = [
+            pltpu.make_async_remote_copy(
                 src_ref=box,
                 dst_ref=msg.at[me],
-                send_sem=all_send,
-                recv_sem=all_recv,
+                send_sem=all_send.at[i],
+                recv_sem=all_recv.at[i],
                 device_id=device,
                 device_id_type=MESH,
-            ).start()
-        )
-
-    stacked = count_z * EXTENT
-    mode = iota((1, modes_z), 1)
-    mode_layer = mode // EXTENT
-    mode_inner = mode - EXTENT * mode_layer
-    tiled = hot(mode_inner == iota((EXTENT, modes_z), 0))
+            )
+            for i, device in enumerate(near_peers())
+        ]
+        for copy in near_copies:
+            copy.start()
+
     diag = choose(ztab[...].reshape(stacked, EXTENT), tiled)
     diag = jnp.where(mode_layer == iota((stacked, modes_z), 0) % count_z, diag, 0.0)
-    zz = iota((span_z, stacked), 0)
-    layer = iota((1, stacked), 1) % count_z
-    inner = iota((1, stacked), 1) // count_z
-    band = hot(zz == SPAN * layer - 1 + inner)
-    near = hot((high(zz) == layer) & (inner == low(zz) + 1))
     hi, lo = split(place(band, diag))
     zfwd[0:span_z, :] = hi
     zfwd[span_z : 2 * span_z, :] = lo
     zfwd[2 * span_z : 3 * span_z, :] = hi
-    eye_z = hot(iota((modes_z, modes_z), 0) == iota((modes_z, modes_z), 1))
     hi, lo = split(turn(eye_z, place(near, diag)))
     zbwd[:, 0:span_z] = hi
     zbwd[:, span_z : 2 * span_z] = lo
@@ -376,6 +380,23 @@
         hi, lo = split(field)
         part[v] = bdot(fwd[:, 0 : 3 * MAIN], jnp.concatenate([hi, lo, hi], axis=0))
 
+    if direct:
+        for copy in near_copies:
+            copy.wait_recv()
+        slab = pl.ds(first * members, near_total)
+        far_copies = [
+            pltpu.make_async_remote_copy(
+                src_ref=msg.at[slab],
+                dst_ref=msg.at[slab],
+                send_sem=all_send.at[near_total - 1 + i],
+                recv_sem=all_recv.at[near_total - 1 + i],
+                device_id=device,
+                device_id_type=MESH,
+            )
+            for i, device in enumerate(far_peers())
+        ]
+        for copy in far_copies:
+            copy.start()
     for copy in halo:
         copy.wait_recv()
 
@@ -418,10 +439,8 @@
 
     updates = None
     if direct:
-        done = pltpu.make_async_copy(
-            msg.at[pl.ds(0, total - 1)], msg.at[pl.ds(0, total - 1)], all_recv
-        )
-        done.wait()
+        for copy in far_copies:
+            copy.wait_recv()
         blocks = msg[...]
         whole = pltpu.roll(jnp.sum(blocks, axis=0), half, 1)
         whole = jnp.where(lane8 < half, whole, 0.0)
@@ -455,9 +474,8 @@
     for copy in halo:
         copy.wait_send()
     if direct:
-        pltpu.make_async_copy(
-            msg.at[pl.ds(0, total - 1)], msg.at[pl.ds(0, total - 1)], all_send
-        ).wait()
+        for copy in near_copies + far_copies:
+            copy.wait_send()
     for store in stores:
         store.wait()
 
@@ -479,6 +497,7 @@
     total = groups * members
     rows, cols = coarse_inverse.shape
     direct = total <= 64 and members == 2 and rows == 8 and cols == 64 and groups * 8 == 128
+    direct = direct and groups % PLANES == 0
     operands = (
         residual,
         jnp.transpose(horiz_vectors, (1, 0, 2)),
@@ -513,8 +532,8 @@
         dma((vectors,)),
         dma((halos,)),
         dma((halos,)),
-        dma,
-        dma,
+        dma((groups // PLANES * members + PLANES,)),
+        dma((groups // PLANES * members + PLANES,)),
     ]
     result = pl.pallas_call(
         functools.partial(kernel, groups, members, direct),

time: 17.2 us -> 18.5 us (1.076)
  Pallas kernels: 15.1 us -> 16.5 us
    pallas_call x1, Pallas kernels: 15.1 us -> 16.5 us  [on_device(): pl.pallas_call(functools.partial(kernel, groups, members, direct), out_sh...]
where the time goes in v3:
time: 18.5 us; the launch traced here: 18.4 us
  Pallas kernels  16.5 us (89%)
  local copies, waits for them, and re-layouts  1.87 us (10%)
    pallas_call x1, Pallas kernels, on_device(): pl.pallas_call(functools.partial(kernel, groups, members, direct), out_sh...  16.5 us
    unnamed x1, local copies, waits for them, and re-layouts  1.87 us

profile of v3, /device:TPU:0, one launch (start us, length us, event | category | flops | bytes accessed | tf_op | source)
XLA Modules:
  0.0 18.4 jit_solution(17389854807103035173)
XLA Ops:
  0.0 16.5 %shard_map.73 = f32[2,16,32,128]{3,2,1,0:T(8,128)} custom-call(f32[2,16,32,128]{3,2,1,0:T(8,128)} %res_hbm.1, f32[18,2,18]{2,1,0:T(2,128)} %bitcast.3, f32[2,18]{1,0:T(2,128)} %hval_hbm.1, f32[18,8,18]{2,1,0:T(8,128)} %bitcast.2, f32[8,18]{1,0:T(8,128)} %zval_hbm.1, s32[1,2,8]{2,1,0:T(2,128)} %agg_hbm.1, f32[8,64]{1,0:T(8,128)} %inv_hbm.1), custom_call_target="tpu_custom_call" | custom-call | flops 2000000000 | bytes 1048576 | tf_op jit(solution)/shard_map/pallas_call | solution.py:538
  16.5 1.9 %copy.9 = f32[2,16,32,128]{3,2,1,0:T(8,128)} copy(f32[2,16,32,128]{3,2,1,0:T(8,128)} %shard_map.73) | data formatting | bytes 1048576

commit v4 on v3

--- a/solution.py
+++ b/solution.py
@@ -14,7 +14,6 @@
 REST = 2 * SPAN + 2 * TAIL
 ROWS = MAIN + REST
 WEIGHT = float(SPAN) ** (-1.5)
-PLANES = 4
 MESH = pl.DeviceIdType.MESH
 F32 = jnp.float32
 BF16 = jnp.bfloat16
@@ -183,21 +182,12 @@
     def shifted(dx, dy):
         return (wrap(g + dx % groups, groups), wrap(m + dy % members, members))
 
-    plane = groups // PLANES
-    first = g // plane * plane
-    inside = g - first
-
-    def near_peers():
-        peers = [(g, wrap(m + dy, members)) for dy in range(1, members)]
-        for dx in range(1, plane):
-            other = first + wrap(inside + dx, plane)
-            peers += [(other, wrap(m + dy, members)) for dy in range(members)]
-        return peers
-
-    def far_peers():
-        return [(wrap(g + plane * dz, groups), m) for dz in range(1, PLANES)]
-
-    near_total = plane * members
+    def peers():
+        found = [(g, wrap(m + dy, members)) for dy in range(1, members)]
+        for dx in range(1, groups):
+            other = wrap(g + dx, groups)
+            found += [(other, wrap(m + dy, members)) for dy in range(members)]
+        return found
 
     barrier = pltpu.get_barrier_semaphore()
     loads = [
@@ -219,9 +209,7 @@
     corner_dy = (1,) if members == 2 else (1, -1)
     around = [(1, 0), (-1, 0), (0, 1)] + [(0, -1)] * (members > 2)
     around += [(dx, dy) for dx in (1, -1) for dy in corner_dy]
-    partners = [shifted(dx, dy) for dx, dy in around]
-    if direct:
-        partners += near_peers() + far_peers()
+    partners = peers() if direct else [shifted(dx, dy) for dx, dy in around]
     for device in partners:
         pl.semaphore_signal(barrier, inc=1, device_id=device, device_id_type=MESH)
     hpad[...] = jnp.zeros_like(hpad)
@@ -250,24 +238,6 @@
     for load in loads[1:]:
         load.wait()
 
-    hpad[0, 0:EXTENT, 0:EXTENT] = hvec[:, 0, :]
-    hpad[1, 0:EXTENT, 0:EXTENT] = hvec[:, 1, :]
-    xe = choose(turn(eye, hpad[0]), px)
-    ye = choose(turn(eye, hpad[1]), py)
-    body = xe[:EXTENT][:, None, :] * ye[:SPAN][None, :, :]
-    table = jnp.concatenate(
-        [
-            body.reshape(EXTENT * SPAN, wide),
-            xe * ye[SPAN : SPAN + 1, :],
-            xe * ye[SPAN + 1 : SPAN + 2, :],
-        ],
-        axis=0,
-    )
-    store_split(fwd, table)
-    xb = choose(hpad[0, 1 : SPAN + 1, 0:TAIL], ma)
-    yb = choose(hpad[1, 1 : SPAN + 1, 0:TAIL], mb)
-    store_split(bwd, (xb[:, None, :] * yb[None, :, :]).reshape(MAIN, wide))
-
     if direct:
         half = inv.shape[1]
         labels = dot(agg[0].astype(F32), spread.astype(F32))
@@ -331,19 +301,37 @@
     for copy in halo:
         copy.start()
     if direct:
-        near_copies = [
+        shares = [
             pltpu.make_async_remote_copy(
                 src_ref=box,
                 dst_ref=msg.at[me],
-                send_sem=all_send.at[i],
-                recv_sem=all_recv.at[i],
+                send_sem=all_send,
+                recv_sem=all_recv,
                 device_id=device,
                 device_id_type=MESH,
             )
-            for i, device in enumerate(near_peers())
+            for device in partners
         ]
-        for copy in near_copies:
+        for copy in shares:
             copy.start()
+
+    hpad[0, 0:EXTENT, 0:EXTENT] = hvec[:, 0, :]
+    hpad[1, 0:EXTENT, 0:EXTENT] = hvec[:, 1, :]
+    xe = choose(turn(eye, hpad[0]), px)
+    ye = choose(turn(eye, hpad[1]), py)
+    body = xe[:EXTENT][:, None, :] * ye[:SPAN][None, :, :]
+    table = jnp.concatenate(
+        [
+            body.reshape(EXTENT * SPAN, wide),
+            xe * ye[SPAN : SPAN + 1, :],
+            xe * ye[SPAN + 1 : SPAN + 2, :],
+        ],
+        axis=0,
+    )
+    store_split(fwd, table)
+    xb = choose(hpad[0, 1 : SPAN + 1, 0:TAIL], ma)
+    yb = choose(hpad[1, 1 : SPAN + 1, 0:TAIL], mb)
+    store_split(bwd, (xb[:, None, :] * yb[None, :, :]).reshape(MAIN, wide))
 
     diag = choose(ztab[...].reshape(stacked, EXTENT), tiled)
     diag = jnp.where(mode_layer == iota((stacked, modes_z), 0) % count_z, diag, 0.0)
@@ -380,23 +368,6 @@
         hi, lo = split(field)
         part[v] = bdot(fwd[:, 0 : 3 * MAIN], jnp.concatenate([hi, lo, hi], axis=0))
 
-    if direct:
-        for copy in near_copies:
-            copy.wait_recv()
-        slab = pl.ds(first * members, near_total)
-        far_copies = [
-            pltpu.make_async_remote_copy(
-                src_ref=msg.at[slab],
-                dst_ref=msg.at[slab],
-                send_sem=all_send.at[near_total - 1 + i],
-                recv_sem=all_recv.at[near_total - 1 + i],
-                device_id=device,
-                device_id_type=MESH,
-            )
-            for i, device in enumerate(far_peers())
-        ]
-        for copy in far_copies:
-            copy.start()
     for copy in halo:
         copy.wait_recv()
 
@@ -439,8 +410,8 @@
 
     updates = None
     if direct:
-        for copy in far_copies:
-            copy.wait_recv()
+        everyone = msg.at[pl.ds(0, total - 1)]
+        pltpu.make_async_copy(everyone, everyone, all_recv).wait()
         blocks = msg[...]
         whole = pltpu.roll(jnp.sum(blocks, axis=0), half, 1)
         whole = jnp.where(lane8 < half, whole, 0.0)
@@ -474,8 +445,7 @@
     for copy in halo:
         copy.wait_send()
     if direct:
-        for copy in near_copies + far_copies:
-            copy.wait_send()
+        pltpu.make_async_copy(everyone, everyone, all_send).wait()
     for store in stores:
         store.wait()
 
@@ -497,7 +467,6 @@
     total = groups * members
     rows, cols = coarse_inverse.shape
     direct = total <= 64 and members == 2 and rows == 8 and cols == 64 and groups * 8 == 128
-    direct = direct and groups % PLANES == 0
     operands = (
         residual,
         jnp.transpose(horiz_vectors, (1, 0, 2)),
@@ -532,8 +501,8 @@
         dma((vectors,)),
         dma((halos,)),
         dma((halos,)),
-        dma((groups // PLANES * members + PLANES,)),
-        dma((groups // PLANES * members + PLANES,)),
+        dma,
+        dma,
     ]
     result = pl.pallas_call(
         functools.partial(kernel, groups, members, direct),

time: 18.5 us -> 16.9 us (0.914)
  Pallas kernels: 16.5 us -> 14.8 us
    pallas_call x1, Pallas kernels: 16.5 us -> 14.8 us  [on_device(): pl.pallas_call(functools.partial(kernel, groups, members, direct), out_sh...]
where the time goes in v4:
time: 16.9 us; the launch traced here: 16.7 us
  Pallas kernels  14.8 us (88%)
  local copies, waits for them, and re-layouts  1.87 us (11%)
    pallas_call x1, Pallas kernels, on_device(): pl.pallas_call(functools.partial(kernel, groups, members, direct), out_sh...  14.8 us
    unnamed x1, local copies, waits for them, and re-layouts  1.87 us

profile of v4, /device:TPU:0, one launch (start us, length us, event | category | flops | bytes accessed | tf_op | source)
XLA Modules:
  0.0 16.7 jit_solution(2688620527593641236)
XLA Ops:
  0.0 14.8 %shard_map.73 = f32[2,16,32,128]{3,2,1,0:T(8,128)} custom-call(f32[2,16,32,128]{3,2,1,0:T(8,128)} %res_hbm.1, f32[18,2,18]{2,1,0:T(2,128)} %bitcast.3, f32[2,18]{1,0:T(2,128)} %hval_hbm.1, f32[18,8,18]{2,1,0:T(8,128)} %bitcast.2, f32[8,18]{1,0:T(8,128)} %zval_hbm.1, s32[1,2,8]{2,1,0:T(2,128)} %agg_hbm.1, f32[8,64]{1,0:T(8,128)} %inv_hbm.1), custom_call_target="tpu_custom_call" | custom-call | flops 2000000000 | bytes 1048576 | tf_op jit(solution)/shard_map/pallas_call | solution.py:507
  14.8 1.9 %copy.9 = f32[2,16,32,128]{3,2,1,0:T(8,128)} copy(f32[2,16,32,128]{3,2,1,0:T(8,128)} %shard_map.73) | data formatting | bytes 1048576

commit v5 on v4

--- a/solution.py
+++ b/solution.py
@@ -242,8 +242,12 @@
         half = inv.shape[1]
         labels = dot(agg[0].astype(F32), spread.astype(F32))
         row_id = iota((2 * half, span_z), 0).astype(F32)
-        member_of = jnp.concatenate(
-            [hot(labels[j : j + 1, :] == row_id) for j in range(count_y)], axis=1
+        member_of = [(labels[j : j + 1, :] == row_id).astype(F32) for j in range(count_y)]
+        downward = hot(high(iota((span_z, count_z), 0)) == iota((span_z, count_z), 1))
+        upright = dot_t(downward.astype(F32), agg[0].astype(F32))
+        lane_id = iota((span_z, 2 * half), 1).astype(F32)
+        owned = jnp.concatenate(
+            [hot(upright[:, j : j + 1] == lane_id) for j in range(count_y)], axis=0
         )
         apad[:, 0:half] = inv[...]
     loads[0].wait()
@@ -268,7 +272,7 @@
                 placed = placed + jnp.where((row8 & 3) == v, tot, 0.0)
             sums.append(placed)
         hi, lo = split(jnp.concatenate(sums, axis=1))
-        rhs = WEIGHT * (bdot_t(hi, member_of) + bdot_t(lo, member_of))
+        rhs = WEIGHT * (bdot(hi, owned) + bdot(lo, owned))
         lane8 = iota((8, 2 * half), 1)
         rhs = jnp.where(row8 < 4, pltpu.roll(rhs, half, 1), rhs)
         mine = apad[...] + jnp.where(lane8 < half, 0.0, rhs)
@@ -343,19 +347,18 @@
     zbwd[:, 0:span_z] = hi
     zbwd[:, span_z : 2 * span_z] = lo
 
-    lane_h = iota((ROWS, EXTENT), 1)
-    row_h = iota((ROWS, EXTENT), 0)
-    t = row_h - EXTENT * SPAN
-    along = jnp.where(t >= TAIL, t - TAIL, t)
-    a_of = jnp.where(t < 0, high(row_h), along)
-    b_of = jnp.where(t < 0, low(row_h), jnp.where(t >= TAIL, SPAN + 1, SPAN))
-    column = jnp.where(lane_h == a_of, hval[0:1, :], 0.0)
-    column = column + jnp.where(lane_h == b_of, hval[1:2, :], 0.0)
-    column = jnp.sum(column, axis=1, keepdims=True)
     levels = dot(zval[...], tiled.astype(F32))
     level_own = mode_layer == iota((count_z, modes_z), 0)
     levels = jnp.sum(jnp.where(level_own, levels, 0.0), axis=0, keepdims=True)
-    recip[...] = 1.0 / (column + levels)
+    upright_eye = (iota((TAIL, EXTENT), 0) == iota((TAIL, EXTENT), 1)).astype(F32)
+    columns = dot_t(upright_eye, hval[...])
+    first = jnp.broadcast_to(columns[:, 0:1], (TAIL, modes_z))
+    second = columns[:, 1:2] + levels
+    body = first[:EXTENT][:, None, :] + second[:SPAN][None, :, :]
+    recip[0 : EXTENT * SPAN, :] = 1.0 / body.reshape(EXTENT * SPAN, modes_z)
+    for side in range(2):
+        rows = slice(EXTENT * SPAN + side * TAIL, EXTENT * SPAN + (side + 1) * TAIL)
+        recip[rows, :] = 1.0 / (first + second[SPAN + side : SPAN + side + 1, :])
 
     for v in range(vectors):
         field = jnp.concatenate(
@@ -397,18 +400,21 @@
             rests.append(jnp.concatenate(pieces, axis=0))
         hi, lo = split(jnp.concatenate(rests, axis=1))
         hat = part[v] + bdot(fwd[:, 3 * MAIN :][:, : 3 * REST], jnp.concatenate([hi, lo, hi], axis=0))
-        backs = []
-        for j in range(count_y):
-            hi, lo = split(hat[:, j * span_z : (j + 1) * span_z])
-            spectral = bdot(jnp.concatenate([hi, hi, lo], axis=1), zfwd[...]) * recip[...]
-            hi, lo = split(spectral)
-            both = bdot(hi, zbwd[...])
-            backs.append(
-                both[:, :span_z] + both[:, span_z:] + bdot(lo, zbwd[:, 0:span_z])
-            )
-        solved.append(jnp.concatenate(backs, axis=1))
-
-    updates = None
+        stack = jnp.concatenate(
+            [hat[:, j * span_z : (j + 1) * span_z] for j in range(count_y)], axis=0
+        )
+        hi, lo = split(stack)
+        spectral = bdot(jnp.concatenate([hi, hi, lo], axis=1), zfwd[...])
+        weight = recip[...]
+        spectral = spectral * jnp.concatenate([weight] * count_y, axis=0)
+        hi, lo = split(spectral)
+        both = bdot(hi, zbwd[...])
+        back = both[:, :span_z] + both[:, span_z:] + bdot(lo, zbwd[:, 0:span_z])
+        solved.append(
+            jnp.concatenate([back[j * ROWS : (j + 1) * ROWS] for j in range(count_y)], axis=1)
+        )
+
+    updates = []
     if direct:
         everyone = msg.at[pl.ds(0, total - 1)]
         pltpu.make_async_copy(everyone, everyone, all_recv).wait()
@@ -416,11 +422,18 @@
         whole = pltpu.roll(jnp.sum(blocks, axis=0), half, 1)
         whole = jnp.where(lane8 < half, whole, 0.0)
         blocks = blocks.reshape(groups, members, 8, 2 * half)
-        answer = jnp.zeros((8, groups * 8), F32)
-        for part_m in range(members):
-            chosen = jnp.where(row8 // 4 == part_m, whole, 0.0)
-            answer = answer + dot_t(chosen, blocks[:, part_m].reshape(groups * 8, 2 * half))
-        updates = WEIGHT * choose(answer, member_of)
+        for v in range(vectors):
+            terms = jnp.zeros((groups, 8, 2 * half), F32)
+            for part_m in range(members):
+                at = 4 * part_m + v
+                terms = terms + blocks[:, part_m] * whole[at : at + 1, :][None]
+            answer = jnp.sum(terms.reshape(groups * 8, 2 * half), axis=1, keepdims=True)
+            updates.append(
+                [
+                    WEIGHT * jnp.sum(answer * member_of[j], axis=0, keepdims=True)
+                    for j in range(count_y)
+                ]
+            )
 
     stores = []
     for v in range(vectors):
@@ -435,8 +448,7 @@
         for j in range(count_y):
             piece = result[:, j * span_z : (j + 1) * span_z]
             if direct:
-                lanes = slice(j * span_z, (j + 1) * span_z)
-                piece = piece + (updates[v : v + 1, lanes] + updates[4 + v : 5 + v, lanes])
+                piece = piece + updates[v][j]
             out[v, :, j * SPAN : (j + 1) * SPAN, :] = piece.reshape(SPAN, SPAN, span_z)
         store = pltpu.make_async_copy(out.at[v], out_hbm.at[v], out_sem.at[v])
         store.start()

time: 16.9 us -> 16.3 us (0.964)
  Pallas kernels: 14.8 us -> 14.2 us
    pallas_call x1, Pallas kernels: 14.8 us -> 14.2 us  [on_device(): pl.pallas_call(functools.partial(kernel, groups, members, direct), out_sh...]
where the time goes in v5:
time: 16.3 us; the launch traced here: 16.1 us
  Pallas kernels  14.2 us (87%)
  local copies, waits for them, and re-layouts  1.87 us (11%)
    pallas_call x1, Pallas kernels, on_device(): pl.pallas_call(functools.partial(kernel, groups, members, direct), out_sh...  14.2 us
    unnamed x1, local copies, waits for them, and re-layouts  1.87 us

profile of v5, /device:TPU:0, one launch (start us, length us, event | category | flops | bytes accessed | tf_op | source)
XLA Modules:
  0.0 16.1 jit_solution(11029612932600778629)
XLA Ops:
  0.0 14.2 %shard_map.73 = f32[2,16,32,128]{3,2,1,0:T(8,128)} custom-call(f32[2,16,32,128]{3,2,1,0:T(8,128)} %res_hbm.1, f32[18,2,18]{2,1,0:T(2,128)} %bitcast.3, f32[2,18]{1,0:T(2,128)} %hval_hbm.1, f32[18,8,18]{2,1,0:T(8,128)} %bitcast.2, f32[8,18]{1,0:T(8,128)} %zval_hbm.1, s32[1,2,8]{2,1,0:T(2,128)} %agg_hbm.1, f32[8,64]{1,0:T(8,128)} %inv_hbm.1), custom_call_target="tpu_custom_call" | custom-call | flops 2000000000 | bytes 1048576 | tf_op jit(solution)/shard_map/pallas_call | solution.py:519
  14.2 1.9 %copy.9 = f32[2,16,32,128]{3,2,1,0:T(8,128)} copy(f32[2,16,32,128]{3,2,1,0:T(8,128)} %shard_map.73) | data formatting | bytes 1048576

commit v6 on v5

--- a/solution.py
+++ b/solution.py
@@ -462,6 +462,25 @@
         store.wait()
 
 
+def hand_over(src, dst, sem):
+    vectors, points_x = src.shape[:2]
+    pieces = sem.shape[0] // vectors
+    depth = points_x // pieces
+    copies = []
+    for v in range(vectors):
+        for i in range(pieces):
+            rows = pl.ds(i * depth, depth)
+            copies.append(
+                pltpu.make_async_copy(
+                    src.at[v, rows], dst.at[v, rows], sem.at[v * pieces + i]
+                )
+            )
+    for copy in copies:
+        copy.start()
+    for copy in copies:
+        copy.wait()
+
+
 def on_device(
     residual,
     horiz_vectors,
@@ -530,7 +549,14 @@
         ),
     )(*operands)
     if direct:
-        return result
+        return pl.pallas_call(
+            hand_over,
+            out_shape=jax.ShapeDtypeStruct(residual.shape, F32),
+            in_specs=[pl.BlockSpec(memory_space=pltpu.HBM)],
+            out_specs=pl.BlockSpec(memory_space=pltpu.HBM),
+            scratch_shapes=[dma((4 * vectors,))],
+            compiler_params=pltpu.CompilerParams(vmem_limit_bytes=60 * 1024 * 1024),
+        )(result)
     totals = residual.reshape(vectors, SPAN, count_y, SPAN, count_z, SPAN).sum(axis=(1, 3, 5))
     labels = aggregate_map.reshape(-1)
     partial_rhs = WEIGHT * jax.ops.segment_sum(

time: 16.3 us -> 31.4 us (1.93)
  Pallas kernels: 14.2 us -> 31.3 us
  local copies, waits for them, and re-layouts: 1.87 us -> 0 us
    pallas_call x0 -> x1, Pallas kernels: none -> 17.1 us  [on_device(): pl.pallas_call(hand_over, out_shape=jax.ShapeDtypeStruct(residual.shape,...]
    unnamed x1 -> x0, local copies, waits for them, and re-layouts: 1.87 us -> none
where the time goes in v6:
time: 31.4 us; the launch traced here: 31.3 us
  Pallas kernels  31.3 us (100%)
    pallas_call x1, Pallas kernels, on_device(): pl.pallas_call(hand_over, out_shape=jax.ShapeDtypeStruct(residual.shape,...  17.1 us
    pallas_call x1, Pallas kernels, on_device(): pl.pallas_call(functools.partial(kernel, groups, members, direct), out_sh...  14.2 us

profile of v6, /device:TPU:0, one launch (start us, length us, event | category | flops | bytes accessed | tf_op | source)
XLA Modules:
  0.0 31.3 jit_solution(5955163356771305911)
XLA Ops:
  0.0 14.2 %shard_map.73.src = f32[2,16,32,128]{3,2,1,0:T(8,128)} custom-call(f32[2,16,32,128]{3,2,1,0:T(8,128)} %res_hbm.1, f32[18,2,18]{2,1,0:T(2,128)} %bitcast.3, f32[2,18]{1,0:T(2,128)} %hval_hbm.1, f32[18,8,18]{2,1,0:T(8,128)} %bitcast.2, f32[8,18]{1,0:T(8,128)} %zval_hbm.1, s32[1,2,8]{2,1,0:T(2,128)} %agg_hbm.1, f32[8,64]{1,0:T(8,128)} %inv_hbm.1), custom_call_target="tpu_custom_call" | custom-call | flops 2000000000 | bytes 1048576 | tf_op jit(solution)/shard_map/pallas_call | solution.py:538
  14.2 17.1 %shard_map.74 = f32[2,16,32,128]{3,2,1,0:T(8,128)} custom-call(f32[2,16,32,128]{3,2,1,0:T(8,128)} %shard_map.73.src), custom_call_target="tpu_custom_call" | custom-call | tf_op jit(solution)/shard_map/pallas_call | solution.py:552

commit v7 on v5

--- a/solution.py
+++ b/solution.py
@@ -250,6 +250,29 @@
             [hot(upright[:, j : j + 1] == lane_id) for j in range(count_y)], axis=0
         )
         apad[:, 0:half] = inv[...]
+    diag = choose(ztab[...].reshape(stacked, EXTENT), tiled)
+    diag = jnp.where(mode_layer == iota((stacked, modes_z), 0) % count_z, diag, 0.0)
+    hi, lo = split(place(band, diag))
+    zfwd[0:span_z, :] = hi
+    zfwd[span_z : 2 * span_z, :] = lo
+    zfwd[2 * span_z : 3 * span_z, :] = hi
+    hi, lo = split(turn(eye_z, place(near, diag)))
+    zbwd[:, 0:span_z] = hi
+    zbwd[:, span_z : 2 * span_z] = lo
+
+    levels = dot(zval[...], tiled.astype(F32))
+    level_own = mode_layer == iota((count_z, modes_z), 0)
+    levels = jnp.sum(jnp.where(level_own, levels, 0.0), axis=0, keepdims=True)
+    upright_eye = (iota((TAIL, EXTENT), 0) == iota((TAIL, EXTENT), 1)).astype(F32)
+    columns = dot_t(upright_eye, hval[...])
+    first = jnp.broadcast_to(columns[:, 0:1], (TAIL, modes_z))
+    second = columns[:, 1:2] + levels
+    body = first[:EXTENT][:, None, :] + second[:SPAN][None, :, :]
+    recip[0 : EXTENT * SPAN, :] = 1.0 / body.reshape(EXTENT * SPAN, modes_z)
+    for side in range(2):
+        rows = slice(EXTENT * SPAN + side * TAIL, EXTENT * SPAN + (side + 1) * TAIL)
+        recip[rows, :] = 1.0 / (first + second[SPAN + side : SPAN + side + 1, :])
+
     loads[0].wait()
 
     for v in range(vectors):
@@ -336,29 +359,6 @@
     xb = choose(hpad[0, 1 : SPAN + 1, 0:TAIL], ma)
     yb = choose(hpad[1, 1 : SPAN + 1, 0:TAIL], mb)
     store_split(bwd, (xb[:, None, :] * yb[None, :, :]).reshape(MAIN, wide))
-
-    diag = choose(ztab[...].reshape(stacked, EXTENT), tiled)
-    diag = jnp.where(mode_layer == iota((stacked, modes_z), 0) % count_z, diag, 0.0)
-    hi, lo = split(place(band, diag))
-    zfwd[0:span_z, :] = hi
-    zfwd[span_z : 2 * span_z, :] = lo
-    zfwd[2 * span_z : 3 * span_z, :] = hi
-    hi, lo = split(turn(eye_z, place(near, diag)))
-    zbwd[:, 0:span_z] = hi
-    zbwd[:, span_z : 2 * span_z] = lo
-
-    levels = dot(zval[...], tiled.astype(F32))
-    level_own = mode_layer == iota((count_z, modes_z), 0)
-    levels = jnp.sum(jnp.where(level_own, levels, 0.0), axis=0, keepdims=True)
-    upright_eye = (iota((TAIL, EXTENT), 0) == iota((TAIL, EXTENT), 1)).astype(F32)
-    columns = dot_t(upright_eye, hval[...])
-    first = jnp.broadcast_to(columns[:, 0:1], (TAIL, modes_z))
-    second = columns[:, 1:2] + levels
-    body = first[:EXTENT][:, None, :] + second[:SPAN][None, :, :]
-    recip[0 : EXTENT * SPAN, :] = 1.0 / body.reshape(EXTENT * SPAN, modes_z)
-    for side in range(2):
-        rows = slice(EXTENT * SPAN + side * TAIL, EXTENT * SPAN + (side + 1) * TAIL)
-        recip[rows, :] = 1.0 / (first + second[SPAN + side : SPAN + side + 1, :])
 
     for v in range(vectors):
         field = jnp.concatenate(
@@ -438,21 +438,26 @@
     stores = []
     for v in range(vectors):
         hi, lo = split(solved[v])
-        result = bdot(
-            bwd[:, 0 : 3 * MAIN],
-            jnp.concatenate([hi[:MAIN], lo[:MAIN], hi[:MAIN]], axis=0),
-        ) + bdot(
-            bwd[:, 3 * MAIN :][:, : 3 * REST],
-            jnp.concatenate([hi[MAIN:], lo[MAIN:], hi[MAIN:]], axis=0),
-        )
-        for j in range(count_y):
-            piece = result[:, j * span_z : (j + 1) * span_z]
-            if direct:
-                piece = piece + updates[v][j]
-            out[v, :, j * SPAN : (j + 1) * SPAN, :] = piece.reshape(SPAN, SPAN, span_z)
-        store = pltpu.make_async_copy(out.at[v], out_hbm.at[v], out_sem.at[v])
-        store.start()
-        stores.append(store)
+        main_part = jnp.concatenate([hi[:MAIN], lo[:MAIN], hi[:MAIN]], axis=0)
+        rest_part = jnp.concatenate([hi[MAIN:], lo[MAIN:], hi[MAIN:]], axis=0)
+        for piece_x in range(2):
+            rows = slice(piece_x * MAIN // 2, (piece_x + 1) * MAIN // 2)
+            points = slice(piece_x * SPAN // 2, (piece_x + 1) * SPAN // 2)
+            result = bdot(bwd[rows, 0 : 3 * MAIN], main_part) + bdot(
+                bwd[rows, 3 * MAIN :][:, : 3 * REST], rest_part
+            )
+            for j in range(count_y):
+                piece = result[:, j * span_z : (j + 1) * span_z]
+                if direct:
+                    piece = piece + updates[v][j]
+                out[v, points, j * SPAN : (j + 1) * SPAN, :] = piece.reshape(
+                    SPAN // 2, SPAN, span_z
+                )
+            store = pltpu.make_async_copy(
+                out.at[v, points], out_hbm.at[v, points], out_sem.at[2 * v + piece_x]
+            )
+            store.start()
+            stores.append(store)
 
     for copy in halo:
         copy.wait_send()
@@ -510,7 +515,7 @@
         pltpu.VMEM((count_z * EXTENT, 2 * span_z), BF16),
         pltpu.VMEM((vectors, ROWS, count_y * span_z), F32),
         dma((len(operands),)),
-        dma((vectors,)),
+        dma((2 * vectors,)),
         dma((halos,)),
         dma((halos,)),
         dma,

time: 16.3 us -> 16.2 us (level)
  no operation moved by 1% of the time
where the time goes in v7:
time: 16.2 us; the launch traced here: 16.1 us
  Pallas kernels  14.2 us (88%)
  local copies, waits for them, and re-layouts  1.87 us (12%)
    pallas_call x1, Pallas kernels, on_device(): pl.pallas_call(functools.partial(kernel, groups, members, direct), out_sh...  14.2 us
    unnamed x1, local copies, waits for them, and re-layouts  1.87 us

profile of v7, /device:TPU:0, one launch (start us, length us, event | category | flops | bytes accessed | tf_op | source)
XLA Modules:
  0.0 16.1 jit_solution(2354593306687342857)
XLA Ops:
  0.0 14.2 %shard_map.73 = f32[2,16,32,128]{3,2,1,0:T(8,128)} custom-call(f32[2,16,32,128]{3,2,1,0:T(8,128)} %res_hbm.1, f32[18,2,18]{2,1,0:T(2,128)} %bitcast.3, f32[2,18]{1,0:T(2,128)} %hval_hbm.1, f32[18,8,18]{2,1,0:T(8,128)} %bitcast.2, f32[8,18]{1,0:T(8,128)} %zval_hbm.1, s32[1,2,8]{2,1,0:T(2,128)} %agg_hbm.1, f32[8,64]{1,0:T(8,128)} %inv_hbm.1), custom_call_target="tpu_custom_call" | custom-call | flops 2000000000 | bytes 1048576 | tf_op jit(solution)/shard_map/pallas_call | solution.py:524
  14.2 1.9 %copy.9 = f32[2,16,32,128]{3,2,1,0:T(8,128)} copy(f32[2,16,32,128]{3,2,1,0:T(8,128)} %shard_map.73) | data formatting | bytes 1048576

commit v8 on v7

--- a/solution.py
+++ b/solution.py
@@ -528,7 +528,7 @@
         out_specs=pl.BlockSpec(memory_space=pl.ANY),
         scratch_shapes=scratch,
         compiler_params=pltpu.CompilerParams(
-            collective_id=0, has_side_effects=True, vmem_limit_bytes=60 * 1024 * 1024
+            collective_id=0, has_side_effects=True, vmem_limit_bytes=40 * 1024 * 1024
         ),
         cost_estimate=pl.CostEstimate(
             flops=2 * 10**9, bytes_accessed=2**20, transcendentals=0

time: 16.2 us -> 21 us (1.30); the launches traced: 16.1 us -> 20.6 us
  local copies, waits for them, and re-layouts: 1.87 us -> 5.51 us
  Pallas kernels: 14.2 us -> 15.1 us
    unnamed x1 -> x15, local copies, waits for them, and re-layouts: 1.87 us -> 5.51 us
    pallas_call x1, Pallas kernels: 14.2 us -> 15.1 us  [on_device(): pl.pallas_call(functools.partial(kernel, groups, members, direct), out_sh...]
where the time goes in v8:
time: 21 us; the launch traced here: 20.6 us
  Pallas kernels  15.1 us (72%)
  local copies, waits for them, and re-layouts  5.51 us (26%)
    pallas_call x1, Pallas kernels, on_device(): pl.pallas_call(functools.partial(kernel, groups, members, direct), out_sh...  15.1 us
    unnamed x15, local copies, waits for them, and re-layouts  5.51 us

profile of v8, /device:TPU:0, one launch (start us, length us, event | category | flops | bytes accessed | tf_op | source)
XLA Modules:
  0.0 20.6 jit_solution(3012633763899910173)
XLA Ops:
  0.0 0.0 copy-start.6
  0.0 0.0 copy-start.5
  0.0 0.7 %copy-done.6 = s32[1,2,8]{2,1,0:T(2,128)S(1)} copy-done((s32[1,2,8]{2,1,0:T(2,128)S(1)}, s32[1,2,8]{2,1,0:T(2,128)}, u32[]{:S(2)}) %copy-start.6) | copy-done | bytes 88
  0.7 0.0 copy-done.5
  0.7 0.0 copy-start
  0.7 1.0 %copy-done = f32[2,16,32,128]{3,2,1,0:T(8,128)S(1)} copy-done((f32[2,16,32,128]{3,2,1,0:T(8,128)S(1)}, f32[2,16,32,128]{3,2,1,0:T(8,128)}, u32[]{:S(2)}) %copy-start) | copy-done | bytes 524312
  1.7 0.0 copy-start.1
  1.7 0.9 %copy-done.1 = f32[8,18,18]{2,0,1:T(8,128)S(1)} copy-done((f32[8,18,18]{2,0,1:T(8,128)S(1)}, f32[8,18,18]{2,0,1:T(8,128)}, u32[]{:S(2)}) %copy-start.1) | copy-done | bytes 10392
  2.6 0.0 copy-start.2
  2.6 0.7 %copy-done.2 = f32[2,18,18]{2,0,1:T(2,128)S(1)} copy-done((f32[2,18,18]{2,0,1:T(2,128)S(1)}, f32[2,18,18]{2,0,1:T(2,128)}, u32[]{:S(2)}) %copy-start.2) | copy-done | bytes 2616
  3.3 0.0 copy-start.3
  3.3 0.7 %copy-done.3 = f32[8,18]{1,0:T(8,128)S(1)} copy-done((f32[8,18]{1,0:T(8,128)S(1)}, f32[8,18]{1,0:T(8,128)}, u32[]{:S(2)}) %copy-start.3) | copy-done | bytes 600
  4.0 0.0 copy-start.4
  4.0 0.7 %copy-done.4 = f32[8,64]{1,0:T(8,128)S(1)} copy-done((f32[8,64]{1,0:T(8,128)S(1)}, f32[8,64]{1,0:T(8,128)}, u32[]{:S(2)}) %copy-start.4) | copy-done | bytes 2072
  4.7 15.1 %shard_map.73 = f32[2,16,32,128]{3,2,1,0:T(8,128)S(1)} custom-call(f32[2,16,32,128]{3,2,1,0:T(8,128)S(1)} %copy-done, f32[18,2,18]{2,1,0:T(2,128)S(1)} %bitcast.3, f32[2,18]{1,0:T(2,128)S(1)} %copy-done.5, f32[18,8,18]{2,1,0:T(8,128)S(1)} %bitcast.2, f32[8,18]{1,0:T(8,128)S(1)} %copy-done.3, s32[1,2,8]{2,1,0:T(2,128)S(1)} %copy-done.6, f32[8,64]{1,0:T(8,128)S(1)} %copy-done.4), custom_call_target="tpu_custom_call" | custom-call | flops 2000000000 | bytes 1048576 | tf_op jit(solution)/shard_map/pallas_call | solution.py:524
  19.8 0.8 %copy.9 = f32[2,16,32,128]{3,2,1,0:T(8,128)} copy(f32[2,16,32,128]{3,2,1,0:T(8,128)S(1)} %shard_map.73) | data formatting | bytes 1048576
Async XLA Ops:
  0.0 0.7 %copy-start.6 = (s32[1,2,8]{2,1,0:T(2,128)S(1)}, s32[1,2,8]{2,1,0:T(2,128)}, u32[]{:S(2)}) copy-start(s32[1,2,8]{2,1,0:T(2,128)} %agg_hbm.1) | copy-start | bytes 196
  0.0 0.7 %copy-start.5 = (f32[2,18]{1,0:T(2,128)S(1)}, f32[2,18]{1,0:T(2,128)}, u32[]{:S(2)}) copy-start(f32[2,18]{1,0:T(2,128)} %hval_hbm.1) | copy-start | bytes 436
  0.7 1.0 %copy-start = (f32[2,16,32,128]{3,2,1,0:T(8,128)S(1)}, f32[2,16,32,128]{3,2,1,0:T(8,128)}, u32[]{:S(2)}) copy-start(f32[2,16,32,128]{3,2,1,0:T(8,128)} %res_hbm.1) | copy-start | bytes 1572868
  1.7 0.9 %copy-start.1 = (f32[8,18,18]{2,0,1:T(8,128)S(1)}, f32[8,18,18]{2,0,1:T(8,128)}, u32[]{:S(2)}) copy-start(f32[8,18,18]{2,0,1:T(8,128)} %param.10) | copy-start | bytes 31108
  2.6 0.7 %copy-start.2 = (f32[2,18,18]{2,0,1:T(2,128)S(1)}, f32[2,18,18]{2,0,1:T(2,128)}, u32[]{:S(2)}) copy-start(f32[2,18,18]{2,0,1:T(2,128)} %param.8) | copy-start | bytes 7780
  3.3 0.7 %copy-start.3 = (f32[8,18]{1,0:T(8,128)S(1)}, f32[8,18]{1,0:T(8,128)}, u32[]{:S(2)}) copy-start(f32[8,18]{1,0:T(8,128)} %zval_hbm.1) | copy-start | bytes 1732
  4.0 0.7 %copy-start.4 = (f32[8,64]{1,0:T(8,128)S(1)}, f32[8,64]{1,0:T(8,128)}, u32[]{:S(2)}) copy-start(f32[8,64]{1,0:T(8,128)} %inv_hbm.1) | copy-start | bytes 6148
